TPU v7x, 32 devices: a whole 2x2x4 slice. The times are simulated.
32 devices in a mesh: lat: 8 (over z, y), lon: 4 (over x, core).
Axes of the slice: x: 2, y: 2, z: 4, core: 2. Of those that a mesh axis runs over, the one named last changes fastest.
Arguments:
- adj_in: float32 [16, 32, 128, 512], P(None, 'lon', 'lat'), may hold values from -6 to 6
- courant_lon: float32 [32, 128, 512], P(None, 'lat', 'lon'), may hold values from 0.2 to 0.95
- courant_lat: float32 [32, 128, 512], P(None, 'lat', 'lon'), may hold values from 0.1 to 0.9
- mass: float32 [32, 128, 512], P(None, 'lat', 'lon'), may hold values from 0.3 to 3
- entrain: float32 [128, 512], P('lat', 'lon'), may hold values from 0.2 to 0.9
- cloud: int32 [2, 128, 512], P(None, 'lat', 'lon'), may hold values from 0 to 31, as said below
- substeps: int32 [128], P('lat'), may hold values from 1 to 8
Outputs:
- adj_out: float32 [16, 32, 128, 512], P(None, None, 'lat', 'lon')
Inputs may be any that keep to these rules, and one draw needn't show every extreme that they name: cloud[0] <= cloud[1] in every column.
All inputs are finite; a program needn't handle non-finite values.
Results may differ from a plain program's by a relative error of at most 0.0001.
Values sent between devices are 32-bit elements; how exact they have to be, the bound alone decides.
No kernel may reach another device: no remote copies, remote signals or barrier semaphores. Data moves between devices by JAX's collectives and lax.ppermute only.
A program may use at most 128 MiB of HBM per device.

v0:
```python
import jax
import jax.numpy as jnp
from jax import lax
from jax.sharding import PartitionSpec as P

MAXSUB = 8


def passed_along(block, axis, distance):
    devices = range(lax.axis_size(axis))
    route = [((i - distance) % len(devices), i) for i in devices]
    return lax.ppermute(block, axis, route)


def shifted(block, axis, distance):
    devices = range(lax.axis_size(axis))
    route = [(i - distance, i) for i in devices if i - distance in devices]
    return lax.ppermute(block, axis, route)


def to_columns(field):
    return lax.all_to_all(field, "lon", split_axis=3, concat_axis=1, tiled=True)


def east_neighbour(field):
    edge = passed_along(field[:, :, :, :1], "lon", -1)
    return jnp.concatenate([field[:, :, :, 1:], edge], axis=3)


def sweep_all(field, courant, substeps, neighbour):

    def sweep_once(index, state):
        active = (index < substeps).astype(jnp.float32)[None, None, :, None]
        return state + active * courant[None] * (neighbour(state) - state)

    return lax.fori_loop(0, MAXSUB, sweep_once, field)


def convect(moved, mass, entrain, cloud):
    levels = jnp.arange(moved.shape[1], dtype=jnp.int32)[:, None, None]
    inside = ((levels >= cloud[0]) & (levels <= cloud[1])).astype(jnp.float32)
    column_mass = jnp.sum(inside * mass, axis=0)
    detrain = entrain * inside * mass / column_mass
    keep_share = 1.0 - entrain * inside
    column_sum = jnp.sum(inside[None] * moved, axis=1)
    return keep_share[None] * moved + detrain[None] * column_sum[:, None]


def body(adj_in, courant_lon, courant_lat, mass, entrain, cloud, substeps):
    tile_rows = substeps.shape[0]
    latitude = lax.axis_index("lat") * tile_rows + jnp.arange(tile_rows, dtype=jnp.int32)
    last_row = tile_rows * lax.axis_size("lat") - 1
    north_rate = courant_lat * (latitude < last_row).astype(jnp.float32)[None, :, None]
    field = to_columns(adj_in)
    field = sweep_all(field, courant_lon, substeps, east_neighbour)
    edge = shifted(field[:, :, :1, :], "lat", -1)
    following = jnp.concatenate([field[:, :, 1:, :], edge], axis=2)
    moved = field + north_rate[None] * (following - field)
    return convect(moved, mass, entrain, cloud)


def solution(mesh):
    return jax.shard_map(
        body,
        mesh=mesh,
        in_specs=(
            P(None, "lon", "lat", None),
            P(None, "lat", "lon"),
            P(None, "lat", "lon"),
            P(None, "lat", "lon"),
            P("lat", "lon"),
            P(None, "lat", "lon"),
            P("lat"),
        ),
        out_specs=P(None, None, "lat", "lon"),
        check_vma=False,
    )
```

profile of v0, /device:TPU:5, one launch (start us, length us, event | category | flops | bytes accessed | tf_op | source)
XLA Modules:
  0.0 556.8 jit_solution(3132968738512226493)
XLA Ops:
  0.0 26.3 %copy.41 = f32[16,8,16,512]{2,1,0,3:T(8,128)} copy(f32[16,8,16,512]{3,2,1,0:T(8,128)} %param.9) | data formatting | bytes 8388608 | tf_op args[0]
  26.3 29.4 %reshape.39 = f32[4,1,262144]{2,1,0:T(1,128)} reshape(f32[512,16,8,16]{3,2,1,0:T(8,128)} %bitcast.11) | data formatting | bytes 8388608
  62.6 46.0 %all-to-all-done = f32[4,1,262144]{2,1,0:T(1,128)} async-done(((f32[4,1,262144]{2,1,0:T(1,128)}), f32[4,1,262144]{2,1,0:T(1,128)}, u32[]{:S(2)}, u32[]{:S(2)}) %all-to-all-start) | async-done | bytes 4194336 | tf_op jit(solution)/shard_map/all_to_all | solution.py:22
  109.2 15.4 %reduce = f32[4,262144]{1,0:T(4,128)} reduce(f32[4,1,262144]{2,1,0:T(1,128)} %all-to-all-done, f32[]{:T(128)} %broadcast.70), dimensions={1}, to_apply=%all_to_all.13.reduce_sub_computation | reduce | bytes 8388612 | tf_op jit(solution)/shard_map/all_to_all | solution.py:22
  124.6 24.9 %reshape.40 = f32[512,16,8,16]{3,2,1,0:T(8,128)} reshape(f32[4,262144]{1,0:T(4,128)} %reduce) | data formatting | bytes 8388608
  149.5 20.6 %copy.51 = f32[16,8,16,4,128]{4,3,2,1,0:T(4,128)} copy(f32[16,8,16,4,128]{2,1,0,4,3:T(8,128)} %bitcast.10) | data formatting | bytes 8388608 | tf_op jit(solution)/shard_map/all_to_all | solution.py:22
  174.8 11.2 %copy.44 = f32[16,32,16,128]{1,2,3,0:T(8,128)} copy(f32[16,32,16,128]{3,2,1,0:T(8,128)} %bitcast.13) | data formatting | bytes 8388608 | tf_op jit(solution)/shard_map/while | solution.py:36
  186.0 335.7 %while.13 = (s32[]{:T(128)}, f32[16,32,16,128]{1,2,3,0:T(8,128)}, s32[16]{0:T(128)S(1)}, f32[32,16,128]{0,1,2:T(8,128)S(1)}, s32[]{:T(128)}) while((s32[]{:T(128)}, f32[16,32,16,128]{1,2,3,0:T(8,128)}, s32[16]{0:T(128)S(1)}, f32[32,16,128]{0,1,2:T(8,128)S(1)}, s32[]{:T(128)}) %tuple.39), condition=%wide.region_1.0_spmd, body=%wide.region_0.0_spmd.sunk | while | flops 4259874 | bytes 39256360 | solution.py:36
  188.0 12.4 %copy.56 = f32[16,32,16,128]{3,2,1,0:T(8,128)} copy(f32[16,32,16,128]{1,2,3,0:T(8,128)} %get-tuple-element.149) | data formatting | bytes 8388608 | tf_op jit(solution)/shard_map
  217.1 11.2 %copy.59 = f32[16,32,16,128]{1,2,3,0:T(8,128)} copy(f32[16,32,16,128]{3,2,1,0:T(8,128)} %fusion.8) | data formatting | bytes 8388608 | tf_op jit(solution)/shard_map
  229.4 12.4 %copy.56 = f32[16,32,16,128]{3,2,1,0:T(8,128)} copy(f32[16,32,16,128]{1,2,3,0:T(8,128)} %get-tuple-element.149) | data formatting | bytes 8388608 | tf_op jit(solution)/shard_map
  258.5 11.2 %copy.59 = f32[16,32,16,128]{1,2,3,0:T(8,128)} copy(f32[16,32,16,128]{3,2,1,0:T(8,128)} %fusion.8) | data formatting | bytes 8388608 | tf_op jit(solution)/shard_map
  271.2 12.4 %copy.56 = f32[16,32,16,128]{3,2,1,0:T(8,128)} copy(f32[16,32,16,128]{1,2,3,0:T(8,128)} %get-tuple-element.149) | data formatting | bytes 8388608 | tf_op jit(solution)/shard_map
  300.3 11.2 %copy.59 = f32[16,32,16,128]{1,2,3,0:T(8,128)} copy(f32[16,32,16,128]{3,2,1,0:T(8,128)} %fusion.8) | data formatting | bytes 8388608 | tf_op jit(solution)/shard_map
  313.5 12.4 %copy.56 = f32[16,32,16,128]{3,2,1,0:T(8,128)} copy(f32[16,32,16,128]{1,2,3,0:T(8,128)} %get-tuple-element.149) | data formatting | bytes 8388608 | tf_op jit(solution)/shard_map
  342.6 11.2 %copy.59 = f32[16,32,16,128]{1,2,3,0:T(8,128)} copy(f32[16,32,16,128]{3,2,1,0:T(8,128)} %fusion.8) | data formatting | bytes 8388608 | tf_op jit(solution)/shard_map
  355.8 12.4 %copy.56 = f32[16,32,16,128]{3,2,1,0:T(8,128)} copy(f32[16,32,16,128]{1,2,3,0:T(8,128)} %get-tuple-element.149) | data formatting | bytes 8388608 | tf_op jit(solution)/shard_map
  384.9 11.2 %copy.59 = f32[16,32,16,128]{1,2,3,0:T(8,128)} copy(f32[16,32,16,128]{3,2,1,0:T(8,128)} %fusion.8) | data formatting | bytes 8388608 | tf_op jit(solution)/shard_map
  397.2 12.4 %copy.56 = f32[16,32,16,128]{3,2,1,0:T(8,128)} copy(f32[16,32,16,128]{1,2,3,0:T(8,128)} %get-tuple-element.149) | data formatting | bytes 8388608 | tf_op jit(solution)/shard_map
  439.1 12.4 %copy.56 = f32[16,32,16,128]{3,2,1,0:T(8,128)} copy(f32[16,32,16,128]{1,2,3,0:T(8,128)} %get-tuple-element.149) | data formatting | bytes 8388608 | tf_op jit(solution)/shard_map
  481.4 12.4 %copy.56 = f32[16,32,16,128]{3,2,1,0:T(8,128)} copy(f32[16,32,16,128]{1,2,3,0:T(8,128)} %get-tuple-element.149) | data formatting | bytes 8388608 | tf_op jit(solution)/shard_map
  510.5 11.2 %copy.59 = f32[16,32,16,128]{1,2,3,0:T(8,128)} copy(f32[16,32,16,128]{3,2,1,0:T(8,128)} %fusion.8) | data formatting | bytes 8388608 | tf_op jit(solution)/shard_map
  521.7 11.9 %copy.47 = f32[16,32,16,128]{3,1,2,0:T(8,128)} copy(f32[16,32,16,128]{1,2,3,0:T(8,128)} %get-tuple-element.84) | data formatting | bytes 8388608 | tf_op jit(solution)/shard_map/while | solution.py:36
  536.6 12.4 %copy.50 = f32[16,32,16,128]{3,2,1,0:T(8,128)} copy(f32[16,32,16,128]{1,2,3,0:T(8,128)} %get-tuple-element.84) | data formatting | bytes 8388608 | tf_op jit(solution)/shard_map/while | solution.py:36
  (105 shorter events, 192.5 us)
Async XLA Ops:
  55.7 5.6 %copy-start.3 = (f32[32,16,128]{2,1,0:T(8,128)S(1)}, f32[32,16,128]{2,1,0:T(8,128)}, u32[]{:S(2)}) copy-start(f32[32,16,128]{2,1,0:T(8,128)} %param.10) | copy-start | bytes 786436
  55.7 6.2 %copy-start.5 = (s32[2,16,128]{2,1,0:T(8,128)S(1)}, s32[2,16,128]{2,1,0:T(8,128)}, u32[]{:S(2)}) copy-start(s32[2,16,128]{2,1,0:T(8,128)} %param.14) | copy-start | bytes 49156
  55.7 6.2 %copy-start.1 = (f32[32,16,128]{2,1,0:T(8,128)S(1)}, f32[32,16,128]{2,1,0:T(8,128)}, u32[]{:S(2)}) copy-start(f32[32,16,128]{2,1,0:T(8,128)} %param.12) | copy-start | bytes 786436
  55.7 53.0 %all-to-all-start = ((f32[4,1,262144]{2,1,0:T(1,128)}), f32[4,1,262144]{2,1,0:T(1,128)}, u32[]{:S(2)}, u32[]{:S(2)}) async-start(f32[4,1,262144]{2,1,0:T(1,128)} %reshape.39), calls=%async_computation | async-start | bytes 8388608 | tf_op jit(solution)/shard_map/all_to_all | solution.py:22
  174.8 11.2 %copy-start.7 = (s32[16]{0:T(128)S(1)}, s32[16]{0:T(128)}, u32[]{:S(2)}) copy-start(s32[16]{0:T(128)} %param.15) | copy-start | bytes 196
  186.9 19.2 %collective-permute-start = (f32[16,32,16,1]{1,2,3,0:T(8,128)S(1)}, f32[16,32,16,1]{1,2,3,0:T(8,128)S(1)}, u32[]{:S(2)}, u32[]{:S(2)}) collective-permute-start(f32[16,32,16,1]{1,2,3,0:T(8,128)S(1)} %slice.37), channel_id=1, source_target_pairs={{1,0},{2,1},{3,2},{0,3},{5,4},{6,5},{7,6},{4,7},{9,8},{10,9},{11,1... | collective-permute-start | bytes 98312 | tf_op jit(solution)/shard_map/while/body/eval_jaxpr/ppermute | solution.py:12
  229.2 18.4 %collective-permute-start = (f32[16,32,16,1]{1,2,3,0:T(8,128)S(1)}, f32[16,32,16,1]{1,2,3,0:T(8,128)S(1)}, u32[]{:S(2)}, u32[]{:S(2)}) collective-permute-start(f32[16,32,16,1]{1,2,3,0:T(8,128)S(1)} %slice.37), channel_id=1, source_target_pairs={{1,0},{2,1},{3,2},{0,3},{5,4},{6,5},{7,6},{4,7},{9,8},{10,9},{11,1... | collective-permute-start | bytes 98312 | tf_op jit(solution)/shard_map/while/body/eval_jaxpr/ppermute | solution.py:12
  270.6 18.8 %collective-permute-start = (f32[16,32,16,1]{1,2,3,0:T(8,128)S(1)}, f32[16,32,16,1]{1,2,3,0:T(8,128)S(1)}, u32[]{:S(2)}, u32[]{:S(2)}) collective-permute-start(f32[16,32,16,1]{1,2,3,0:T(8,128)S(1)} %slice.37), channel_id=1, source_target_pairs={{1,0},{2,1},{3,2},{0,3},{5,4},{6,5},{7,6},{4,7},{9,8},{10,9},{11,1... | collective-permute-start | bytes 98312 | tf_op jit(solution)/shard_map/while/body/eval_jaxpr/ppermute | solution.py:12
  312.4 19.3 %collective-permute-start = (f32[16,32,16,1]{1,2,3,0:T(8,128)S(1)}, f32[16,32,16,1]{1,2,3,0:T(8,128)S(1)}, u32[]{:S(2)}, u32[]{:S(2)}) collective-permute-start(f32[16,32,16,1]{1,2,3,0:T(8,128)S(1)} %slice.37), channel_id=1, source_target_pairs={{1,0},{2,1},{3,2},{0,3},{5,4},{6,5},{7,6},{4,7},{9,8},{10,9},{11,1... | collective-permute-start | bytes 98312 | tf_op jit(solution)/shard_map/while/body/eval_jaxpr/ppermute | solution.py:12
  354.7 19.2 %collective-permute-start = (f32[16,32,16,1]{1,2,3,0:T(8,128)S(1)}, f32[16,32,16,1]{1,2,3,0:T(8,128)S(1)}, u32[]{:S(2)}, u32[]{:S(2)}) collective-permute-start(f32[16,32,16,1]{1,2,3,0:T(8,128)S(1)} %slice.37), channel_id=1, source_target_pairs={{1,0},{2,1},{3,2},{0,3},{5,4},{6,5},{7,6},{4,7},{9,8},{10,9},{11,1... | collective-permute-start | bytes 98312 | tf_op jit(solution)/shard_map/while/body/eval_jaxpr/ppermute | solution.py:12
  397.0 18.4 %collective-permute-start = (f32[16,32,16,1]{1,2,3,0:T(8,128)S(1)}, f32[16,32,16,1]{1,2,3,0:T(8,128)S(1)}, u32[]{:S(2)}, u32[]{:S(2)}) collective-permute-start(f32[16,32,16,1]{1,2,3,0:T(8,128)S(1)} %slice.37), channel_id=1, source_target_pairs={{1,0},{2,1},{3,2},{0,3},{5,4},{6,5},{7,6},{4,7},{9,8},{10,9},{11,1... | collective-permute-start | bytes 98312 | tf_op jit(solution)/shard_map/while/body/eval_jaxpr/ppermute | solution.py:12
  438.4 18.8 %collective-permute-start = (f32[16,32,16,1]{1,2,3,0:T(8,128)S(1)}, f32[16,32,16,1]{1,2,3,0:T(8,128)S(1)}, u32[]{:S(2)}, u32[]{:S(2)}) collective-permute-start(f32[16,32,16,1]{1,2,3,0:T(8,128)S(1)} %slice.37), channel_id=1, source_target_pairs={{1,0},{2,1},{3,2},{0,3},{5,4},{6,5},{7,6},{4,7},{9,8},{10,9},{11,1... | collective-permute-start | bytes 98312 | tf_op jit(solution)/shard_map/while/body/eval_jaxpr/ppermute | solution.py:12
  480.3 19.3 %collective-permute-start = (f32[16,32,16,1]{1,2,3,0:T(8,128)S(1)}, f32[16,32,16,1]{1,2,3,0:T(8,128)S(1)}, u32[]{:S(2)}, u32[]{:S(2)}) collective-permute-start(f32[16,32,16,1]{1,2,3,0:T(8,128)S(1)} %slice.37), channel_id=1, source_target_pairs={{1,0},{2,1},{3,2},{0,3},{5,4},{6,5},{7,6},{4,7},{9,8},{10,9},{11,1... | collective-permute-start | bytes 98312 | tf_op jit(solution)/shard_map/while/body/eval_jaxpr/ppermute | solution.py:12
  521.7 14.9 %copy-start.4 = (f32[32,16,128]{2,1,0:T(8,128)S(1)}, f32[32,16,128]{2,1,0:T(8,128)}, u32[]{:S(2)}) copy-start(f32[32,16,128]{2,1,0:T(8,128)} %param.11) | copy-start | bytes 786436
  521.7 14.9 %copy-start.6 = (f32[16,128]{1,0:T(8,128)S(1)}, f32[16,128]{1,0:T(8,128)}, u32[]{:S(2)}) copy-start(f32[16,128]{1,0:T(8,128)} %param.13) | copy-start | bytes 24580
  534.6 17.2 %collective-permute-start.1 = (f32[16,32,1,128]{3,1,2,0:T(8,128)S(1)}, f32[16,32,1,128]{3,1,2,0:T(8,128)S(1)}, u32[]{:S(2)}, u32[]{:S(2)}) collective-permute-start(f32[16,32,1,128]{3,1,2,0:T(8,128)S(1)} %slice.32), channel_id=1, source_target_pairs={{4,0},{8,4},{12,8},{16,12},{20,16},{24,20},{28,24},{5,1},{9,5},{13... | collective-permute-start | bytes 786440 | tf_op jit(solution)/shard_map/ppermute | solution.py:18
  549.0 3.4 copy-start
  549.0 3.5 copy-start.2
where the time goes:
time: 563 us; the launch traced here: 557 us
  local copies, waits for them, and re-layouts  413 us (73%)
  other arithmetic  85.1 us (15%)
  waiting for transfers between devices  46.1 us (8%)
  starting transfers between devices  12.4 us (2%)
    another operation x16, local copies, waits for them, and re-layouts  188 us
    unnamed x19, local copies, waits for them, and re-layouts  81.3 us
    add x8, other arithmetic, sweep_once(): return state + active * courant[None] * (neighbour(state) - state)  63.3 us
    all_to_all x1, waiting for transfers between devices, to_columns(): return lax.all_to_all(field, 'lon', split_axis=3, concat_axis=1, tiled=True)  46 us
    slice x8, local copies, waits for them, and re-layouts, east_neighbour(): return jnp.concatenate([field[:, :, :, 1:], edge], axis=3)  42.4 us
    while x4, local copies, waits for them, and re-layouts, sweep_all(): return lax.fori_loop(0, MAXSUB, sweep_once, field)  36 us
    all_to_all x3, local copies, waits for them, and re-layouts, to_columns(): return lax.all_to_all(field, 'lon', split_axis=3, concat_axis=1, tiled=True)  25.8 us
    ppermute x8, local copies, waits for them, and re-layouts, passed_along(): return lax.ppermute(block, axis, route)  24.1 us
  transfers between devices with their start and end apart: 10, of which 1 were waited for; matrix products, arithmetic and copies ran while one was open for 29% of the time, Pallas kernels for 0%

commit v1 on v0

v1 whole, which is shorter than its diff:
```python
import jax
import jax.numpy as jnp
from jax import lax
from jax.experimental import pallas as pl
from jax.experimental.pallas import tpu as pltpu
from jax.sharding import PartitionSpec as P

MAXSUB = 8
HALF = 8
VMEM_LIMIT = 48 * 1024 * 1024


def sent_east(block, distance):
    n = lax.axis_size("lon")
    return lax.ppermute(block, "lon", [(i, (i + distance) % n) for i in range(n)])


def sent_south(block):
    n = lax.axis_size("lat")
    return lax.ppermute(block, "lat", [(i + 1, i) for i in range(n - 1)])


def call(kernel, grid, in_specs, out_specs, out_shape, operands, scalars, elements, aliases=None, scratch=()):
    return pl.pallas_call(
        kernel,
        grid_spec=pltpu.PrefetchScalarGridSpec(
            num_scalar_prefetch=1, grid=grid, in_specs=in_specs, out_specs=out_specs, scratch_shapes=scratch
        ),
        out_shape=out_shape,
        input_output_aliases=aliases or {},
        compiler_params=pltpu.CompilerParams(vmem_limit_bytes=VMEM_LIMIT),
        cost_estimate=pl.CostEstimate(flops=elements * 20, bytes_accessed=elements * 8, transcendentals=0),
    )(scalars, *operands)


def sweep(me, adj, rates, active, moments, step, level_block, skip, row_block):
    n = len(rates)
    width = rates[0].shape[2]
    first, count = moments
    levels = rates[0].shape[0]
    rows = row_block[1]

    def kernel(me_ref, *refs):
        fields, cs, act, outs = refs[:n], refs[n : 2 * n], refs[2 * n], refs[2 * n + 1 :]
        last = lax.broadcasted_iota(jnp.int32, (levels, HALF, width), 2) == width - 1

        def one(m, carry):
            for g in range(rows // HALF):
                part = slice(g * HALF, (g + 1) * HALF)
                steps = jnp.broadcast_to(act[part, :][None], (levels, HALF, width))
                state = [f[m, skip : skip + levels, part, :] for f in fields]
                for s in range(MAXSUB):
                    rolled = [pltpu.roll(a, width - 1, 2) for a in state]
                    state = [
                        a
                        + jnp.where(steps > s, c[:, part, :], 0.0)
                        * (jnp.where(last, rolled[(r + 1) % n], rolled[r]) - a)
                        for r, (a, c) in enumerate(zip(state, cs))
                    ]
                for a, o in zip(state, outs):
                    o[m, :, part, :] = a
            return carry

        lax.fori_loop(0, step, one, 0)

    def tile(r):
        return pl.BlockSpec(
            (step, level_block, rows, width),
            lambda i, me, r=r: (i + first // step, 0, row_block[0], lax.rem(me[0] + r, n)),
        )

    in_specs = [tile(r) for r in range(n)]
    in_specs += [pl.BlockSpec((levels, rows, width), lambda i, me: (0, row_block[0], 0))] * n
    in_specs += [pl.BlockSpec((rows, width), lambda i, me: (row_block[0], 0))]
    out_specs = [pl.BlockSpec((step, levels, rows, width), lambda i, me: (i, 0, 0, 0))] * n
    out_shape = [jax.ShapeDtypeStruct((count, levels, rows, width), jnp.float32)] * n
    return call(
        kernel, (count // step,), in_specs, out_specs, out_shape, [adj] * n + list(rates) + [active], me,
        count * levels * rows * width * n,
    )


def coefficients(me, courant_lat, mass, entrain, cloud, north, n):
    levels, rows, width = mass.shape
    share = levels // n

    def kernel(me_ref, lat_ref, mass_ref, entrain_ref, cloud_ref, north_ref, rate_ref, inside_ref, detrain_ref):
        total = jnp.zeros((rows, width), jnp.float32)
        base, top = cloud_ref[0], cloud_ref[1]
        for r in range(n):
            owner = lax.rem(me_ref[0] - r + n, n)
            for l in range(share):
                level = owner * share + l
                inside = jnp.where((level >= base) & (level <= top), 1.0, 0.0)
                air = inside * mass_ref[level]
                total = total + air
                inside_ref[r * share + l] = inside
                detrain_ref[r * share + l] = air
                rate_ref[r * share + l] = lat_ref[level] * north_ref[...]
        factor = entrain_ref[...] / total
        for l in range(levels):
            detrain_ref[l] = detrain_ref[l] * factor

    full = pl.BlockSpec((levels, rows, width), lambda i, me: (0, 0, 0))
    flat = pl.BlockSpec((rows, width), lambda i, me: (0, 0))
    return call(
        kernel, (1,), [full, full, flat, pl.BlockSpec((2, rows, width), lambda i, me: (0, 0, 0)), flat],
        [full] * 3, [jax.ShapeDtypeStruct((levels, rows, width), jnp.float32)] * 3,
        [courant_lat, mass, entrain, cloud, north], me, levels * rows * width,
    )


def south_rows(me, tops, souths, step):
    n = len(tops)
    count, first, _, width = tops[0].shape
    rest = souths[0].shape[1]
    share = first + rest

    def kernel(me_ref, *refs):
        a, b, o = refs[:n], refs[n : 2 * n], refs[2 * n]

        def one(m, carry):
            for r in range(n):
                for l in range(first):
                    o[m, r * share + l : r * share + l + 1, :] = a[r][m, l, :1, :]
                for l in range(rest):
                    k = r * share + first + l
                    o[m, k : k + 1, :] = b[r][m, l, :1, :]
            return carry

        lax.fori_loop(0, step, one, 0)

    in_specs = [pl.BlockSpec((step, first, HALF, width), lambda i, me: (i, 0, 0, 0))] * n
    in_specs += [pl.BlockSpec((step, rest, HALF, width), lambda i, me: (i, 0, 0, 0))] * n
    return call(
        kernel, (count // step,), in_specs, pl.BlockSpec((step, n * share, width), lambda i, me: (i, 0, 0)),
        jax.ShapeDtypeStruct((count, n * share, width), jnp.float32), list(tops) + list(souths), me,
        count * n * share * width * HALF,
    )


def finish(me, out, first_moment, tops, souths, norths, edges, rate, inside, detrain, entrain, step):
    n = len(tops)
    total_moments, first, rows, width = tops[0].shape
    count, rest = norths[0].shape[:2]
    share = first + rest
    levels = n * share
    base = first_moment // step

    def kernel(me_ref, *refs):
        a, b, c = refs[:n], refs[n : 2 * n], refs[2 * n : 3 * n]
        edge_ref, rate_ref, inside_ref, detrain_ref, entrain_ref = refs[3 * n : 3 * n + 5]
        o = refs[-1]
        top_row = lax.broadcasted_iota(jnp.int32, (HALF, width), 0) == HALF - 1
        low, high = slice(0, HALF), slice(HALF, 2 * HALF)

        def one(m, carry):
            sums = [jnp.zeros((HALF, width), jnp.float32), jnp.zeros((HALF, width), jnp.float32)]
            for r in range(n):
                owner = lax.rem(me_ref[0] - r + n, n)
                for l in range(share):
                    k = r * share + l
                    if l < first:
                        f0, f1 = a[r][m, l, low, :], a[r][m, l, high, :]
                    else:
                        f0, f1 = b[r][m, l - first], c[r][m, l - first]
                    up0, up1 = pltpu.roll(f0, HALF - 1, 0), pltpu.roll(f1, HALF - 1, 0)
                    edge = jnp.broadcast_to(edge_ref[m, k : k + 1, :], (HALF, width))
                    n0, n1 = jnp.where(top_row, up1, up0), jnp.where(top_row, edge, up1)
                    m0 = f0 + rate_ref[k, low, :] * (n0 - f0)
                    m1 = f1 + rate_ref[k, high, :] * (n1 - f1)
                    sums[0] = sums[0] + inside_ref[k, low, :] * m0
                    sums[1] = sums[1] + inside_ref[k, high, :] * m1
                    o[m, owner * share + l, low, :] = m0
                    o[m, owner * share + l, high, :] = m1
            for r in range(n):
                owner = lax.rem(me_ref[0] - r + n, n)
                for l in range(share):
                    k = r * share + l
                    for part, whole in ((low, sums[0]), (high, sums[1])):
                        keep = 1.0 - entrain_ref[part, :] * inside_ref[k, part, :]
                        moved = o[m, owner * share + l, part, :]
                        o[m, owner * share + l, part, :] = keep * moved + detrain_ref[k, part, :] * whole
            return carry

        lax.fori_loop(0, step, one, 0)

    full = pl.BlockSpec((levels, rows, width), lambda i, me: (0, 0, 0))
    in_specs = [pl.BlockSpec((step, first, rows, width), lambda i, me: (i + base, 0, 0, 0))] * n
    in_specs += [pl.BlockSpec((step, rest, HALF, width), lambda i, me: (i + base, 0, 0, 0))] * n
    in_specs += [pl.BlockSpec((step, rest, HALF, width), lambda i, me: (i, 0, 0, 0))] * n
    in_specs += [pl.BlockSpec((step, levels, width), lambda i, me: (i + base, 0, 0))]
    in_specs += [full] * 3 + [pl.BlockSpec((rows, width), lambda i, me: (0, 0))]
    operands = list(tops) + list(souths) + list(norths) + [edges, rate, inside, detrain, entrain]
    aliases = None
    if out is not None:
        in_specs.append(pl.BlockSpec(memory_space=pl.ANY))
        operands.append(out)
        aliases = {len(operands): 0}
    return call(
        kernel, (count // step,), in_specs,
        pl.BlockSpec((step, levels, rows, width), lambda i, me: (i + base, 0, 0, 0)),
        jax.ShapeDtypeStruct((total_moments, levels, rows, width), jnp.float32), operands, me,
        count * levels * rows * width, aliases,
    )


CHUNKS = (8, 4, 2, 1, 1)


def body(adj_in, courant_lon, courant_lat, mass, entrain, cloud, substeps):
    n = lax.axis_size("lon")
    moments, share, rows, _ = adj_in.shape
    width = courant_lon.shape[2]
    position = lax.axis_index("lon").astype(jnp.int32)
    me = position[None]
    first, rest = 1, share - 1

    def rates_of(start, size, r):
        dest = lax.rem(position - r + n, n)
        block = lax.dynamic_slice_in_dim(courant_lon, dest * share + start, size, 0)
        return sent_east(block, n - r) if r else block

    active = jnp.broadcast_to(substeps[:, None], (rows, width))
    latitude = lax.axis_index("lat") * rows + jnp.arange(rows, dtype=jnp.int32)
    north = (latitude < rows * lax.axis_size("lat") - 1).astype(jnp.float32)
    north = jnp.broadcast_to(north[:, None], (rows, width))

    rates_a = [rates_of(0, first, r) for r in range(n)]
    rates_b = [rates_of(first, rest, r) for r in range(n)]

    def exchanged(blocks):
        return [blocks[0]] + [sent_east(blocks[r], r) for r in range(1, n)]

    tops = exchanged(sweep(me, adj_in, rates_a, active, (0, moments), 8, first, 0, (0, rows)))
    souths = exchanged(sweep(me, adj_in, rates_b, active, (0, moments), 4, share, first, (0, HALF)))
    norths, start = [], 0
    for size in CHUNKS:
        norths.append(
            exchanged(sweep(me, adj_in, rates_b, active, (start, size), min(size, 4), share, first, (1, HALF)))
        )
        start += size

    rate, inside, detrain = coefficients(me, courant_lat, mass, entrain, cloud, north, n)
    edges = sent_south(south_rows(me, tops, souths, 8))
    out, start = None, 0
    for size, chunk in zip(CHUNKS, norths):
        out = finish(
            me, out, start, tops, souths, chunk, edges, rate, inside, detrain, entrain, min(size, 2)
        )
        start += size
    return out


def solution(mesh):
    return jax.shard_map(
        body,
        mesh=mesh,
        in_specs=(
            P(None, "lon", "lat", None),
            P(None, "lat", "lon"),
            P(None, "lat", "lon"),
            P(None, "lat", "lon"),
            P("lat", "lon"),
            P(None, "lat", "lon"),
            P("lat"),
        ),
        out_specs=P(None, None, "lat", "lon"),
        check_vma=False,
    )
```

time: 563 us -> 111 us (0.20)
  local copies, waits for them, and re-layouts: 413 us -> 11.2 us
  other arithmetic: 85.1 us -> 0.01 us
  Pallas kernels: 0 us -> 43.7 us
  waiting for transfers between devices: 46.1 us -> 27.6 us
  starting transfers between devices: 12.4 us -> 25.7 us
    another operation x16 -> x0, local copies, waits for them, and re-layouts: 188 us -> none
    unnamed x19 -> x46, local copies, waits for them, and re-layouts: 81.3 us -> 8.78 us
    add x9 -> x0, other arithmetic: 66.5 us -> none  [the longest x8 63.3 us: sweep_once(): return state + active * courant[None] * (neighbour(state) - state)]
    slice x18 -> x0, local copies, waits for them, and re-layouts: 53.5 us -> none  [the longest x8 42.4 us: east_neighbour(): return jnp.concatenate([field[:, :, :, 1:], edge], axis=3)]
    all_to_all x1 -> x0, waiting for transfers between devices: 46 us -> none  [to_columns(): return lax.all_to_all(field, 'lon', split_axis=3, concat_axis=1, tiled=True)]
    pallas_call x0 -> x14, Pallas kernels: none -> 43.7 us  [call(): pl.pallas_call(kernel, grid_spec=pltpu.PrefetchScalarGridSpec(num_scalar_...]
    while x4 -> x0, local copies, waits for them, and re-layouts: 36 us -> none  [sweep_all(): return lax.fori_loop(0, MAXSUB, sweep_once, field)]
    ppermute x9 -> x28, waiting for transfers between devices: 0.02 us -> 27.6 us  [the longest x27 27.6 us: sent_east(): lax.ppermute(block, 'lon', [(i, (i + distance) % n) for i in range(n)])]
  transfers between devices with their start and end apart: 10 -> 28, of which waited for: 1 -> 7; matrix products, arithmetic and copies ran while one was open for 29% -> 1% of each run, Pallas kernels for 0% -> 28%
where the time goes in v1:
time: 111 us; the launch traced here: 108 us
  Pallas kernels  43.7 us (39%)
  waiting for transfers between devices  27.6 us (25%)
  starting transfers between devices  25.7 us (23%)
  local copies, waits for them, and re-layouts  11.2 us (10%)
    pallas_call x14, Pallas kernels, call(): pl.pallas_call(kernel, grid_spec=pltpu.PrefetchScalarGridSpec(num_scalar_...  43.7 us
    ppermute x27, waiting for transfers between devices, sent_east(): lax.ppermute(block, 'lon', [(i, (i + distance) % n) for i in range(n)])  27.6 us
    ppermute x27, starting transfers between devices, sent_east(): lax.ppermute(block, 'lon', [(i, (i + distance) % n) for i in range(n)])  23.6 us
    unnamed x46, local copies, waits for them, and re-layouts  8.78 us
  transfers between devices with their start and end apart: 28, of which 7 were waited for; matrix products, arithmetic and copies ran while one was open for 1% of the time, Pallas kernels for 28%

profile of v1, /device:TPU:5, one launch (start us, length us, event | category | flops | bytes accessed | tf_op | source)
XLA Modules:
  0.0 108.5 jit_solution(6834209095934338164)
XLA Ops:
  1.6 1.2 %collective-permute-start.7 = (f32[7,16,128]{2,1,0:T(8,128)S(1)}, f32[7,16,128]{2,1,0:T(8,128)S(1)}, u32[]{:S(2)}, u32[]{:S(2)}) collective-permute-start(f32[7,16,128]{2,1,0:T(8,128)S(1)} %get-tuple-element.70), channel_id=1, source_target_pairs={{0,2},{1,3},{2,0},{3,1},{4,6},{5,7},{6,4},{7,5},{8,10},{9,11},{10,... | collective-permute-start | bytes 172040 | tf_op jit(solution)/shard_map/ppermute | solution.py:15
  2.9 1.3 %collective-permute-start.8 = (f32[7,16,128]{2,1,0:T(8,128)S(1)}, f32[7,16,128]{2,1,0:T(8,128)S(1)}, u32[]{:S(2)}, u32[]{:S(2)}) collective-permute-start(f32[7,16,128]{2,1,0:T(8,128)S(1)} %get-tuple-element.67), channel_id=1, source_target_pairs={{0,1},{1,2},{2,3},{3,0},{4,5},{5,6},{6,7},{7,4},{8,9},{9,10},{10,1... | collective-permute-start | bytes 172040 | tf_op jit(solution)/shard_map/ppermute | solution.py:15
  6.4 12.5 %shard_map.74 = (f32[16,7,8,128]{3,2,1,0:T(8,128)S(1)}, f32[16,7,8,128]{3,2,1,0:T(8,128)}, f32[16,7,8,128]{3,2,1,0:T(8,128)S(1)}, f32[16,7,8,128]{3,2,1,0:T(8,128)}) custom-call(s32[1]{0:T(128)} %bitcast.me_ref, f32[16,8,16,512]{3,2,1,0:T(8,128)} %refs_3_.13, f32[16,8,16,512]{3,2,1,0:T(8,128)} %refs_3_.13, f32[16,8,16,512]{3,2,1,0:T(8,128)} %refs_3_.13, ...), custom_call_target="tpu_custom_call" | custom-call | flops 9175040 | bytes 3670016 | tf_op jit(solution)/shard_map/pallas_call | solution.py:24
  19.0 1.1 %collective-permute-start.10 = (f32[16,7,8,128]{3,2,1,0:T(8,128)S(1)}, f32[16,7,8,128]{3,2,1,0:T(8,128)S(1)}, u32[]{:S(2)}, u32[]{:S(2)}) collective-permute-start(f32[16,7,8,128]{3,2,1,0:T(8,128)S(1)} %get-tuple-element.42), channel_id=1, source_target_pairs={{0,2},{1,3},{2,0},{3,1},{4,6},{5,7},{6,4},{7,5},{8,10},{9,11},{10,... | collective-permute-start | bytes 1376264 | tf_op jit(solution)/shard_map/ppermute | solution.py:15
  20.1 1.8 %collective-permute-start.11 = (f32[16,7,8,128]{3,2,1,0:T(8,128)}, f32[16,7,8,128]{3,2,1,0:T(8,128)S(1)}, u32[]{:S(2)}, u32[]{:S(2)}) collective-permute-start(f32[16,7,8,128]{3,2,1,0:T(8,128)} %get-tuple-element.43), channel_id=1, source_target_pairs={{0,3},{1,0},{2,1},{3,2},{4,7},{5,4},{6,5},{7,6},{8,11},{9,8},{10,9... | collective-permute-start | bytes 1376264 | tf_op jit(solution)/shard_map/ppermute | solution.py:15
  24.0 17.2 %collective-permute-done.refs_5_ = f32[1,16,128]{2,1,0:T(8,128)S(1)} collective-permute-done((f32[1,16,128]{2,1,0:T(8,128)S(1)}, f32[1,16,128]{2,1,0:T(8,128)S(1)}, u32[]{:S(2)}, u32[]{:S(2)}) %collective-permute-start) | collective-permute-done | bytes 8224 | tf_op jit(solution)/shard_map/ppermute | solution.py:15
  41.2 1.2 %collective-permute-done.2.refs_7_ = f32[1,16,128]{2,1,0:T(8,128)S(1)} collective-permute-done((f32[1,16,128]{2,1,0:T(8,128)S(1)}, f32[1,16,128]{2,1,0:T(8,128)S(1)}, u32[]{:S(2)}, u32[]{:S(2)}) %collective-permute-start.2) | collective-permute-done | bytes 8224 | tf_op jit(solution)/shard_map/ppermute | solution.py:15
  42.4 2.2 %copy-done = f32[16,8,16,512]{3,2,1,0:T(8,128)S(1)} copy-done((f32[16,8,16,512]{3,2,1,0:T(8,128)S(1)}, f32[16,8,16,512]{3,2,1,0:T(8,128)}, u32[]{:S(2)}) %copy-start) | copy-done | bytes 4194328
  44.6 9.5 %shard_map.73 = (f32[16,1,16,128]{3,2,1,0:T(8,128)S(1)}, f32[16,1,16,128]{3,2,1,0:T(8,128)S(1)}, f32[16,1,16,128]{3,2,1,0:T(8,128)S(1)}, f32[16,1,16,128]{3,2,1,0:T(8,128)S(1)}) custom-call(s32[1]{0:T(128)} %bitcast.me_ref, f32[16,8,16,512]{3,2,1,0:T(8,128)S(1)} %copy-done, f32[16,8,16,512]{3,2,1,0:T(8,128)S(1)} %copy-done, f32[16,8,16,512]{3,2,1,0:T(8,128)S(1)} %copy-done, ...), custom_call_target="tpu_custom_call" | custom-call | flops 2621440 | bytes 1048576 | tf_op jit(solution)/shard_map/pallas_call | solution.py:24
  54.1 2.0 %collective-permute-start.3 = (f32[16,1,16,128]{3,2,1,0:T(8,128)S(1)}, f32[16,1,16,128]{3,2,1,0:T(8,128)S(1)}, u32[]{:S(2)}, u32[]{:S(2)}) collective-permute-start(f32[16,1,16,128]{3,2,1,0:T(8,128)S(1)} %get-tuple-element.37), channel_id=1, source_target_pairs={{0,1},{1,2},{2,3},{3,0},{4,5},{5,6},{6,7},{7,4},{8,9},{9,10},{10,1... | collective-permute-start | bytes 393224 | tf_op jit(solution)/shard_map/ppermute | solution.py:15
  57.2 1.6 %collective-permute-done.3.refs_1_ = f32[16,1,16,128]{3,2,1,0:T(8,128)S(1)} collective-permute-done((f32[16,1,16,128]{3,2,1,0:T(8,128)S(1)}, f32[16,1,16,128]{3,2,1,0:T(8,128)S(1)}, u32[]{:S(2)}, u32[]{:S(2)}) %collective-permute-start.3) | collective-permute-done | bytes 131104 | tf_op jit(solution)/shard_map/ppermute | solution.py:15
  58.8 2.2 %collective-permute-start.5 = (f32[16,1,16,128]{3,2,1,0:T(8,128)S(1)}, f32[16,1,16,128]{3,2,1,0:T(8,128)S(1)}, u32[]{:S(2)}, u32[]{:S(2)}) collective-permute-start(f32[16,1,16,128]{3,2,1,0:T(8,128)S(1)} %get-tuple-element.39), channel_id=1, source_target_pairs={{0,3},{1,0},{2,1},{3,2},{4,7},{5,4},{6,5},{7,6},{8,11},{9,8},{10,9... | collective-permute-start | bytes 393224 | tf_op jit(solution)/shard_map/ppermute | solution.py:15
  61.0 3.3 %shard_map.80 = (f32[4,7,8,128]{3,2,1,0:T(8,128)S(1)}, f32[4,7,8,128]{3,2,1,0:T(8,128)S(1)}, f32[4,7,8,128]{3,2,1,0:T(8,128)S(1)}, f32[4,7,8,128]{3,2,1,0:T(8,128)}) custom-call(s32[1]{0:T(128)} %bitcast.me_ref, f32[16,8,16,512]{3,2,1,0:T(8,128)S(1)} %copy-done, f32[16,8,16,512]{3,2,1,0:T(8,128)S(1)} %copy-done, f32[16,8,16,512]{3,2,1,0:T(8,128)S(1)} %copy-done, ...), custom_call_target="tpu_custom_call" | custom-call | flops 2293760 | bytes 917504 | tf_op jit(solution)/shard_map/pallas_call | solution.py:24
  66.4 1.3 %shard_map.79 = (f32[2,7,8,128]{3,2,1,0:T(8,128)S(1)}, f32[2,7,8,128]{3,2,1,0:T(8,128)S(1)}, f32[2,7,8,128]{3,2,1,0:T(8,128)S(1)}, f32[2,7,8,128]{3,2,1,0:T(8,128)S(1)}) custom-call(s32[1]{0:T(128)} %bitcast.me_ref, f32[16,8,16,512]{3,2,1,0:T(8,128)S(1)} %copy-done, f32[16,8,16,512]{3,2,1,0:T(8,128)S(1)} %copy-done, f32[16,8,16,512]{3,2,1,0:T(8,128)S(1)} %copy-done, ...), custom_call_target="tpu_custom_call" | custom-call | flops 1146880 | bytes 458752 | tf_op jit(solution)/shard_map/pallas_call | solution.py:24
  70.7 2.1 %collective-permute-start.15 = (f32[16,32,128]{2,1,0:T(8,128)S(1)}, f32[16,32,128]{2,1,0:T(8,128)S(1)}, u32[]{:S(2)}, u32[]{:S(2)}) collective-permute-start(f32[16,32,128]{2,1,0:T(8,128)S(1)} %shard_map.76), channel_id=1, source_target_pairs={{4,0},{8,4},{12,8},{16,12},{20,16},{24,20},{28,24},{5,1},{9,5},{13... | collective-permute-start | bytes 786440 | tf_op jit(solution)/shard_map/ppermute | solution.py:20
  74.0 6.3 %shard_map.81 = (f32[8,7,8,128]{3,2,1,0:T(8,128)S(1)}, f32[8,7,8,128]{3,2,1,0:T(8,128)}, f32[8,7,8,128]{3,2,1,0:T(8,128)}, f32[8,7,8,128]{3,2,1,0:T(8,128)}) custom-call(s32[1]{0:T(128)} %bitcast.me_ref, f32[16,8,16,512]{3,2,1,0:T(8,128)S(1)} %copy-done.1, f32[16,8,16,512]{3,2,1,0:T(8,128)S(1)} %copy-done.1, f32[16,8,16,512]{3,2,1,0:T(8,128)S(1)} %copy-done.1, ...), custom_call_target="tpu_custom_call" | custom-call | flops 4587520 | bytes 1835008 | tf_op jit(solution)/shard_map/pallas_call | solution.py:24
  80.9 2.3 %collective-permute-start.25 = (f32[8,7,8,128]{3,2,1,0:T(8,128)}, f32[8,7,8,128]{3,2,1,0:T(8,128)}, u32[]{:S(2)}, u32[]{:S(2)}) collective-permute-start(f32[8,7,8,128]{3,2,1,0:T(8,128)} %get-tuple-element.64), channel_id=1, source_target_pairs={{0,1},{1,2},{2,3},{3,0},{4,5},{5,6},{6,7},{7,4},{8,9},{9,10},{10,1... | collective-permute-start | bytes 688136 | tf_op jit(solution)/shard_map/ppermute | solution.py:15
  85.5 1.5 %collective-permute-start.24 = (f32[4,7,8,128]{3,2,1,0:T(8,128)}, f32[4,7,8,128]{3,2,1,0:T(8,128)}, u32[]{:S(2)}, u32[]{:S(2)}) collective-permute-start(f32[4,7,8,128]{3,2,1,0:T(8,128)} %get-tuple-element.62), channel_id=1, source_target_pairs={{0,3},{1,0},{2,1},{3,2},{4,7},{5,4},{6,5},{7,6},{8,11},{9,8},{10,9... | collective-permute-start | bytes 344072 | tf_op jit(solution)/shard_map/ppermute | solution.py:15
  87.0 2.2 %copy-done.2 = f32[16,8,16,512]{3,2,1,0:T(8,128)S(1)} copy-done((f32[16,8,16,512]{3,2,1,0:T(8,128)S(1)}, f32[16,8,16,512]{3,2,1,0:T(8,128)}, u32[]{:S(2)}) %copy-start.2) | copy-done | bytes 4194328
  89.9 6.0 %collective-permute-done.24.refs_11_ = f32[4,7,8,128]{3,2,1,0:T(8,128)} collective-permute-done((f32[4,7,8,128]{3,2,1,0:T(8,128)}, f32[4,7,8,128]{3,2,1,0:T(8,128)}, u32[]{:S(2)}, u32[]{:S(2)}) %collective-permute-start.24) | collective-permute-done | bytes 114720 | tf_op jit(solution)/shard_map/ppermute | solution.py:15
  95.9 1.1 %collective-permute-start.17 = (f32[1,7,8,128]{3,2,1,0:T(8,128)S(1)}, f32[1,7,8,128]{3,2,1,0:T(8,128)S(1)}, u32[]{:S(2)}, u32[]{:S(2)}) collective-permute-start(f32[1,7,8,128]{3,2,1,0:T(8,128)S(1)} %copy-done.22), channel_id=1, source_target_pairs={{0,2},{1,3},{2,0},{3,1},{4,6},{5,7},{6,4},{7,5},{8,10},{9,11},{10,... | collective-permute-start | bytes 86024 | tf_op jit(solution)/shard_map/ppermute | solution.py:15
  97.0 1.7 %collective-permute-start.12 = (f32[1,7,8,128]{3,2,1,0:T(8,128)S(1)}, f32[1,7,8,128]{3,2,1,0:T(8,128)S(1)}, u32[]{:S(2)}, u32[]{:S(2)}) collective-permute-start(f32[1,7,8,128]{3,2,1,0:T(8,128)S(1)} %get-tuple-element.45), channel_id=1, source_target_pairs={{0,1},{1,2},{2,3},{3,0},{4,5},{5,6},{6,7},{7,4},{8,9},{9,10},{10,1... | collective-permute-start | bytes 86024 | tf_op jit(solution)/shard_map/ppermute | solution.py:15
  99.5 3.9 %shard_map.82.refs_17_ = f32[16,32,16,128]{3,2,1,0:T(8,128)} custom-call(s32[1]{0:T(128)} %bitcast.me_ref, f32[16,1,16,128]{3,2,1,0:T(8,128)S(1)} %get-tuple-element.36.refs_0_, f32[16,1,16,128]{3,2,1,0:T(8,128)S(1)} %collective-permute-done.3.refs_1_, f32[16,1,16,128]{3,2,1,0:T(8,128)S(1)} %collective-permute-done.4.refs_2_, ...), custom_call_target="tpu_custom_call" | custom-call | flops 10485760 | bytes 4194304 | tf_op jit(solution)/shard_map/pallas_call | solution.py:24
  103.5 2.2 %shard_map.83.refs_17_ = f32[16,32,16,128]{3,2,1,0:T(8,128)} custom-call(s32[1]{0:T(128)} %bitcast.me_ref, f32[16,1,16,128]{3,2,1,0:T(8,128)S(1)} %get-tuple-element.36.refs_0_, f32[16,1,16,128]{3,2,1,0:T(8,128)S(1)} %collective-permute-done.3.refs_1_, f32[16,1,16,128]{3,2,1,0:T(8,128)S(1)} %collective-permute-done.4.refs_2_, ...), custom_call_target="tpu_custom_call", output_to_operand_aliasing={{}: (18, {})} | custom-call | flops 5242880 | bytes 2097152 | tf_op jit(solution)/shard_map/pallas_call | solution.py:24
  (97 shorter events, 20.4 us)
Async XLA Ops:
  0.9 4.2 %collective-permute-start.6 = (f32[7,16,128]{2,1,0:T(8,128)S(1)}, f32[7,16,128]{2,1,0:T(8,128)S(1)}, u32[]{:S(2)}, u32[]{:S(2)}) collective-permute-start(f32[7,16,128]{2,1,0:T(8,128)S(1)} %get-tuple-element.68), channel_id=1, source_target_pairs={{0,3},{1,0},{2,1},{3,2},{4,7},{5,4},{6,5},{7,6},{8,11},{9,8},{10,9... | collective-permute-start | bytes 172040 | tf_op jit(solution)/shard_map/ppermute | solution.py:15
  19.0 48.8 %collective-permute-start.10 = (f32[16,7,8,128]{3,2,1,0:T(8,128)S(1)}, f32[16,7,8,128]{3,2,1,0:T(8,128)S(1)}, u32[]{:S(2)}, u32[]{:S(2)}) collective-permute-start(f32[16,7,8,128]{3,2,1,0:T(8,128)S(1)} %get-tuple-element.42), channel_id=1, source_target_pairs={{0,2},{1,3},{2,0},{3,1},{4,6},{5,7},{6,4},{7,5},{8,10},{9,11},{10,... | collective-permute-start | bytes 1376264 | tf_op jit(solution)/shard_map/ppermute | solution.py:15
  20.1 48.7 %collective-permute-start.11 = (f32[16,7,8,128]{3,2,1,0:T(8,128)}, f32[16,7,8,128]{3,2,1,0:T(8,128)S(1)}, u32[]{:S(2)}, u32[]{:S(2)}) collective-permute-start(f32[16,7,8,128]{3,2,1,0:T(8,128)} %get-tuple-element.43), channel_id=1, source_target_pairs={{0,3},{1,0},{2,1},{3,2},{4,7},{5,4},{6,5},{7,6},{8,11},{9,8},{10,9... | collective-permute-start | bytes 1376264 | tf_op jit(solution)/shard_map/ppermute | solution.py:15
  21.8 47.3 %collective-permute-start.9 = (f32[16,7,8,128]{3,2,1,0:T(8,128)}, f32[16,7,8,128]{3,2,1,0:T(8,128)S(1)}, u32[]{:S(2)}, u32[]{:S(2)}) collective-permute-start(f32[16,7,8,128]{3,2,1,0:T(8,128)} %get-tuple-element.41), channel_id=1, source_target_pairs={{0,1},{1,2},{2,3},{3,0},{4,5},{5,6},{6,7},{7,4},{8,9},{9,10},{10,1... | collective-permute-start | bytes 1376264 | tf_op jit(solution)/shard_map/ppermute | solution.py:15
  23.0 18.2 %collective-permute-start = (f32[1,16,128]{2,1,0:T(8,128)S(1)}, f32[1,16,128]{2,1,0:T(8,128)S(1)}, u32[]{:S(2)}, u32[]{:S(2)}) collective-permute-start(f32[1,16,128]{2,1,0:T(8,128)S(1)} %get-tuple-element.73), channel_id=1, source_target_pairs={{0,3},{1,0},{2,1},{3,2},{4,7},{5,4},{6,5},{7,6},{8,11},{9,8},{10,9... | collective-permute-start | bytes 24584 | tf_op jit(solution)/shard_map/ppermute | solution.py:15
  23.1 18.1 %collective-permute-start.1 = (f32[1,16,128]{2,1,0:T(8,128)S(1)}, f32[1,16,128]{2,1,0:T(8,128)S(1)}, u32[]{:S(2)}, u32[]{:S(2)}) collective-permute-start(f32[1,16,128]{2,1,0:T(8,128)S(1)} %get-tuple-element.72), channel_id=1, source_target_pairs={{0,2},{1,3},{2,0},{3,1},{4,6},{5,7},{6,4},{7,5},{8,10},{9,11},{10,... | collective-permute-start | bytes 24584 | tf_op jit(solution)/shard_map/ppermute | solution.py:15
  54.1 4.7 %collective-permute-start.3 = (f32[16,1,16,128]{3,2,1,0:T(8,128)S(1)}, f32[16,1,16,128]{3,2,1,0:T(8,128)S(1)}, u32[]{:S(2)}, u32[]{:S(2)}) collective-permute-start(f32[16,1,16,128]{3,2,1,0:T(8,128)S(1)} %get-tuple-element.37), channel_id=1, source_target_pairs={{0,1},{1,2},{2,3},{3,0},{4,5},{5,6},{6,7},{7,4},{8,9},{9,10},{10,1... | collective-permute-start | bytes 393224 | tf_op jit(solution)/shard_map/ppermute | solution.py:15
  56.1 8.3 %collective-permute-start.4 = (f32[16,1,16,128]{3,2,1,0:T(8,128)S(1)}, f32[16,1,16,128]{3,2,1,0:T(8,128)S(1)}, u32[]{:S(2)}, u32[]{:S(2)}) collective-permute-start(f32[16,1,16,128]{3,2,1,0:T(8,128)S(1)} %get-tuple-element.38), channel_id=1, source_target_pairs={{0,2},{1,3},{2,0},{3,1},{4,6},{5,7},{6,4},{7,5},{8,10},{9,11},{10,... | collective-permute-start | bytes 393224 | tf_op jit(solution)/shard_map/ppermute | solution.py:15
  58.8 7.1 %collective-permute-start.5 = (f32[16,1,16,128]{3,2,1,0:T(8,128)S(1)}, f32[16,1,16,128]{3,2,1,0:T(8,128)S(1)}, u32[]{:S(2)}, u32[]{:S(2)}) collective-permute-start(f32[16,1,16,128]{3,2,1,0:T(8,128)S(1)} %get-tuple-element.39), channel_id=1, source_target_pairs={{0,3},{1,0},{2,1},{3,2},{4,7},{5,4},{6,5},{7,6},{8,11},{9,8},{10,9... | collective-permute-start | bytes 393224 | tf_op jit(solution)/shard_map/ppermute | solution.py:15
  64.3 19.9 %collective-permute-start.22 = (f32[4,7,8,128]{3,2,1,0:T(8,128)S(1)}, f32[4,7,8,128]{3,2,1,0:T(8,128)S(1)}, u32[]{:S(2)}, u32[]{:S(2)}) collective-permute-start(f32[4,7,8,128]{3,2,1,0:T(8,128)S(1)} %get-tuple-element.60), channel_id=1, source_target_pairs={{0,1},{1,2},{2,3},{3,0},{4,5},{5,6},{6,7},{7,4},{8,9},{9,10},{10,1... | collective-permute-start | bytes 344072 | tf_op jit(solution)/shard_map/ppermute | solution.py:15
  67.8 5.1 %collective-permute-start.19 = (f32[2,7,8,128]{3,2,1,0:T(8,128)S(1)}, f32[2,7,8,128]{3,2,1,0:T(8,128)S(1)}, u32[]{:S(2)}, u32[]{:S(2)}) collective-permute-start(f32[2,7,8,128]{3,2,1,0:T(8,128)S(1)} %get-tuple-element.56), channel_id=1, source_target_pairs={{0,1},{1,2},{2,3},{3,0},{4,5},{5,6},{6,7},{7,4},{8,9},{9,10},{10,1... | collective-permute-start | bytes 172040 | tf_op jit(solution)/shard_map/ppermute | solution.py:15
  68.8 11.5 %collective-permute-start.20 = (f32[2,7,8,128]{3,2,1,0:T(8,128)S(1)}, f32[2,7,8,128]{3,2,1,0:T(8,128)S(1)}, u32[]{:S(2)}, u32[]{:S(2)}) collective-permute-start(f32[2,7,8,128]{3,2,1,0:T(8,128)S(1)} %get-tuple-element.57), channel_id=1, source_target_pairs={{0,2},{1,3},{2,0},{3,1},{4,6},{5,7},{6,4},{7,5},{8,10},{9,11},{10,... | collective-permute-start | bytes 172040 | tf_op jit(solution)/shard_map/ppermute | solution.py:15
  69.2 14.1 %collective-permute-start.21 = (f32[2,7,8,128]{3,2,1,0:T(8,128)S(1)}, f32[2,7,8,128]{3,2,1,0:T(8,128)S(1)}, u32[]{:S(2)}, u32[]{:S(2)}) collective-permute-start(f32[2,7,8,128]{3,2,1,0:T(8,128)S(1)} %get-tuple-element.58), channel_id=1, source_target_pairs={{0,3},{1,0},{2,1},{3,2},{4,7},{5,4},{6,5},{7,6},{8,11},{9,8},{10,9... | collective-permute-start | bytes 172040 | tf_op jit(solution)/shard_map/ppermute | solution.py:15
  70.7 28.5 %collective-permute-start.15 = (f32[16,32,128]{2,1,0:T(8,128)S(1)}, f32[16,32,128]{2,1,0:T(8,128)S(1)}, u32[]{:S(2)}, u32[]{:S(2)}) collective-permute-start(f32[16,32,128]{2,1,0:T(8,128)S(1)} %shard_map.76), channel_id=1, source_target_pairs={{4,0},{8,4},{12,8},{16,12},{20,16},{24,20},{28,24},{5,1},{9,5},{13... | collective-permute-start | bytes 786440 | tf_op jit(solution)/shard_map/ppermute | solution.py:20
  73.5 11.4 %collective-permute-start.23 = (f32[4,7,8,128]{3,2,1,0:T(8,128)S(1)}, f32[4,7,8,128]{3,2,1,0:T(8,128)S(1)}, u32[]{:S(2)}, u32[]{:S(2)}) collective-permute-start(f32[4,7,8,128]{3,2,1,0:T(8,128)S(1)} %get-tuple-element.61), channel_id=1, source_target_pairs={{0,2},{1,3},{2,0},{3,1},{4,6},{5,7},{6,4},{7,5},{8,10},{9,11},{10,... | collective-permute-start | bytes 344072 | tf_op jit(solution)/shard_map/ppermute | solution.py:15
  80.9 16.1 %collective-permute-start.25 = (f32[8,7,8,128]{3,2,1,0:T(8,128)}, f32[8,7,8,128]{3,2,1,0:T(8,128)}, u32[]{:S(2)}, u32[]{:S(2)}) collective-permute-start(f32[8,7,8,128]{3,2,1,0:T(8,128)} %get-tuple-element.64), channel_id=1, source_target_pairs={{0,1},{1,2},{2,3},{3,0},{4,5},{5,6},{6,7},{7,4},{8,9},{9,10},{10,1... | collective-permute-start | bytes 688136 | tf_op jit(solution)/shard_map/ppermute | solution.py:15
  83.9 13.2 %collective-permute-start.26 = (f32[8,7,8,128]{3,2,1,0:T(8,128)}, f32[8,7,8,128]{3,2,1,0:T(8,128)}, u32[]{:S(2)}, u32[]{:S(2)}) collective-permute-start(f32[8,7,8,128]{3,2,1,0:T(8,128)} %get-tuple-element.65), channel_id=1, source_target_pairs={{0,2},{1,3},{2,0},{3,1},{4,6},{5,7},{6,4},{7,5},{8,10},{9,11},{10,... | collective-permute-start | bytes 688136 | tf_op jit(solution)/shard_map/ppermute | solution.py:15
  84.9 13.9 %collective-permute-start.27 = (f32[8,7,8,128]{3,2,1,0:T(8,128)}, f32[8,7,8,128]{3,2,1,0:T(8,128)}, u32[]{:S(2)}, u32[]{:S(2)}) collective-permute-start(f32[8,7,8,128]{3,2,1,0:T(8,128)} %get-tuple-element.66), channel_id=1, source_target_pairs={{0,3},{1,0},{2,1},{3,2},{4,7},{5,4},{6,5},{7,6},{8,11},{9,8},{10,9... | collective-permute-start | bytes 688136 | tf_op jit(solution)/shard_map/ppermute | solution.py:15
  85.5 10.4 %collective-permute-start.24 = (f32[4,7,8,128]{3,2,1,0:T(8,128)}, f32[4,7,8,128]{3,2,1,0:T(8,128)}, u32[]{:S(2)}, u32[]{:S(2)}) collective-permute-start(f32[4,7,8,128]{3,2,1,0:T(8,128)} %get-tuple-element.62), channel_id=1, source_target_pairs={{0,3},{1,0},{2,1},{3,2},{4,7},{5,4},{6,5},{7,6},{8,11},{9,8},{10,9... | collective-permute-start | bytes 344072 | tf_op jit(solution)/shard_map/ppermute | solution.py:15
  95.9 10.8 %collective-permute-start.17 = (f32[1,7,8,128]{3,2,1,0:T(8,128)S(1)}, f32[1,7,8,128]{3,2,1,0:T(8,128)S(1)}, u32[]{:S(2)}, u32[]{:S(2)}) collective-permute-start(f32[1,7,8,128]{3,2,1,0:T(8,128)S(1)} %copy-done.22), channel_id=1, source_target_pairs={{0,2},{1,3},{2,0},{3,1},{4,6},{5,7},{6,4},{7,5},{8,10},{9,11},{10,... | collective-permute-start | bytes 86024 | tf_op jit(solution)/shard_map/ppermute | solution.py:15
  97.0 9.7 %collective-permute-start.18 = (f32[1,7,8,128]{3,2,1,0:T(8,128)S(1)}, f32[1,7,8,128]{3,2,1,0:T(8,128)S(1)}, u32[]{:S(2)}, u32[]{:S(2)}) collective-permute-start(f32[1,7,8,128]{3,2,1,0:T(8,128)S(1)} %copy-done.20), channel_id=1, source_target_pairs={{0,3},{1,0},{2,1},{3,2},{4,7},{5,4},{6,5},{7,6},{8,11},{9,8},{10,9... | collective-permute-start | bytes 86024 | tf_op jit(solution)/shard_map/ppermute | solution.py:15
  97.0 10.6 %collective-permute-start.12 = (f32[1,7,8,128]{3,2,1,0:T(8,128)S(1)}, f32[1,7,8,128]{3,2,1,0:T(8,128)S(1)}, u32[]{:S(2)}, u32[]{:S(2)}) collective-permute-start(f32[1,7,8,128]{3,2,1,0:T(8,128)S(1)} %get-tuple-element.45), channel_id=1, source_target_pairs={{0,1},{1,2},{2,3},{3,0},{4,5},{5,6},{6,7},{7,4},{8,9},{9,10},{10,1... | collective-permute-start | bytes 86024 | tf_op jit(solution)/shard_map/ppermute | solution.py:15
  98.8 8.8 %collective-permute-start.13 = (f32[1,7,8,128]{3,2,1,0:T(8,128)S(1)}, f32[1,7,8,128]{3,2,1,0:T(8,128)S(1)}, u32[]{:S(2)}, u32[]{:S(2)}) collective-permute-start(f32[1,7,8,128]{3,2,1,0:T(8,128)S(1)} %get-tuple-element.46), channel_id=1, source_target_pairs={{0,2},{1,3},{2,0},{3,1},{4,6},{5,7},{6,4},{7,5},{8,10},{9,11},{10,... | collective-permute-start | bytes 86024 | tf_op jit(solution)/shard_map/ppermute | solution.py:15
  99.2 8.5 %collective-permute-start.14 = (f32[1,7,8,128]{3,2,1,0:T(8,128)S(1)}, f32[1,7,8,128]{3,2,1,0:T(8,128)S(1)}, u32[]{:S(2)}, u32[]{:S(2)}) collective-permute-start(f32[1,7,8,128]{3,2,1,0:T(8,128)S(1)} %get-tuple-element.47), channel_id=1, source_target_pairs={{0,3},{1,0},{2,1},{3,2},{4,7},{5,4},{6,5},{7,6},{8,11},{9,8},{10,9... | collective-permute-start | bytes 86024 | tf_op jit(solution)/shard_map/ppermute | solution.py:15
  (27 other events, 100.9 us)

commit v2 on v0

v2 whole, which is shorter than its diff:
```python
import functools

import jax
import jax.numpy as jnp
from jax import lax
from jax.experimental import pallas as pl
from jax.experimental.pallas import tpu as pltpu
from jax.sharding import PartitionSpec as P

MAXSUB = 8
HALF = 8
VMEM_LIMIT = 12 * 1024 * 1024
COST = 1024
STENCIL_COST = 2 * 10**8
FIRST = 8
VMEM_WIDE = 50 * 1024 * 1024
NORTH_CHUNKS = (8, 6, 2)


def swapped(block, r):
    n = lax.axis_size("lon")
    return lax.ppermute(block, "lon", [(i, i ^ r) for i in range(n)])


def sent_west(block):
    n = lax.axis_size("lon")
    return lax.ppermute(block, "lon", [(i, (i - 1) % n) for i in range(n)])


def sent_south(block):
    n = lax.axis_size("lat")
    return lax.ppermute(block, "lat", [(i + 1, i) for i in range(n - 1)])


def f32(*shape):
    return jax.ShapeDtypeStruct(shape, jnp.float32)


SCALAR = pl.BlockSpec(memory_space=pltpu.SMEM)
NEAR = pl.BlockSpec(memory_space=pltpu.VMEM)
FAR = pl.BlockSpec(memory_space=pltpu.HBM)
ANY = pl.BlockSpec(memory_space=pl.ANY)


def call(kernel, in_specs, operands, out_specs, out_shape, flops, moved, aliases=None, scratch=(), limit=VMEM_LIMIT, grid=(), cost=None):
    return pl.pallas_call(
        kernel,
        in_specs=in_specs,
        out_specs=out_specs,
        out_shape=out_shape,
        grid=grid,
        scratch_shapes=list(scratch),
        input_output_aliases=aliases or {},
        compiler_params=pltpu.CompilerParams(vmem_limit_bytes=limit),
        cost_estimate=pl.CostEstimate(flops=min(flops, cost or COST), bytes_accessed=cost or min(moved, COST), transcendentals=0),
    )(*operands)


def tile_of(adj, me_ref, r, width, first, count, rows):
    start = pl.multiple_of((me_ref[0] ^ r) * width, width)
    return adj.at[pl.ds(first, count), :, rows, pl.ds(start, width)]


def held_for(block, token):
    def kernel(b, t, o):
        pass

    return call(kernel, [ANY, ANY], [block, token], ANY, f32(*block.shape), 0, 0, {0: 0})


def packed_rates(me, courant):
    levels, rows, width = courant.shape
    per = width // MAXSUB

    def kernel(c, o):
        lane = lax.broadcasted_iota(jnp.int32, (rows, width), 1)
        for b in range(levels // per):
            total = jnp.where(lane < MAXSUB, c[b * per], 0.0)
            for l in range(1, per):
                total = total + pltpu.roll(jnp.where(lane < MAXSUB, c[b * per + l], 0.0), MAXSUB * l, 1)
            o[b] = total

    size = levels * rows * width
    return call(kernel, [NEAR], [courant], NEAR, f32(levels // per, rows, width), size * 3, size * 4)


def taken(me, adj, width, parts, *tokens):
    share = adj.shape[1]

    def kernel(me_ref, a, *refs):
        outs, sems = refs[len(tokens) : -1], refs[-1]
        copies = [
            pltpu.make_async_copy(tile_of(a, me_ref, r, width, first, count, rows), o, sems.at[i])
            for i, ((r, first, count, rows), o) in enumerate(zip(parts, outs))
        ]
        for copy in copies:
            copy.start()
        for copy in copies:
            copy.wait()

    shapes = [f32(count, share, rows.stop - rows.start, width) for _, _, count, rows in parts]
    return call(
        kernel, [SCALAR, FAR] + [ANY] * len(tokens), [me, adj, *tokens], [NEAR] * len(shapes), shapes, 1024, 1024, None,
        [pltpu.SemaphoreType.DMA((len(parts),))], VMEM_WIDE,
    )


def prepared(me, adj, width, n, *tokens):
    moments, share, rows, _ = adj.shape
    step = 4
    many = n - 2
    extra = rows // HALF
    rest = moments - FIRST

    def kernel(me_ref, a, *refs):
        halo, near, *refs = refs[len(tokens) :]
        fars, (tiles, sems, tile_sems) = refs[:many], refs[many:]
        tile_copies = []
        for part in range(moments // step):
            for t in range(n):
                source = a.at[pl.ds(part * step, step), :, :, pl.ds(t * width, width)]
                copy = pltpu.make_async_copy(source, tiles.at[t, pl.ds(part * step, step)], tile_sems.at[part, t])
                copy.start()
                tile_copies.append(copy)
        pairs = [(tile_of(a, me_ref, 1, width, 0, moments, slice(0, rows)), near.at[pl.ds(0, moments)])]
        for r, far in enumerate(fars, 2):
            pairs.append((tile_of(a, me_ref, r, width, FIRST, rest, slice(0, HALF)), far.at[pl.ds(0, rest)]))
        copies = [pltpu.make_async_copy(source, o, sems.at[i]) for i, (source, o) in enumerate(pairs)]
        for copy in copies:
            copy.start()
        lane = lax.broadcasted_iota(jnp.int32, (share, rows, width), 2)
        for copy in tile_copies:
            copy.wait()
        for r in range(n):
            east = lax.rem((me_ref[0] ^ r) + 1, n)
            total = jnp.zeros((share, rows, width), jnp.float32)
            for m in range(moments):
                kept = jnp.where(lane < MAXSUB, tiles[east, m], 0.0)
                total = total + pltpu.roll(kept, MAXSUB * m, 2)
            if r == 0:
                halo[0] = total
            elif r == 1:
                near[moments] = total
            else:
                for g in range(extra):
                    fars[r - 2][rest + g] = total[:, g * HALF : (g + 1) * HALF, :]
        for copy in copies:
            copy.wait()

    shapes = [f32(1, share, rows, width), f32(moments + 1, share, rows, width)]
    shapes += [f32(rest + extra, share, HALF, width)] * many
    return call(
        kernel, [SCALAR, FAR] + [ANY] * len(tokens), [me, adj, *tokens], [NEAR] * len(shapes), shapes, 1024, 1024, None,
        [
            pltpu.VMEM((n, moments, share, rows, width), jnp.float32),
            pltpu.SemaphoreType.DMA((len(shapes),)),
            pltpu.SemaphoreType.DMA((moments // step, n)),
        ],
        VMEM_WIDE,
    )


def stencil(me, courant, halo, active, n, *tokens):
    levels, rows, width = courant.shape
    share = levels // n
    per = width // MAXSUB

    def kernel(me_ref, c_ref, h_ref, act_ref, *refs):
        w_ref, p_ref = refs[len(tokens) :]
        lane = lax.broadcasted_iota(jnp.int32, (rows, width), 1)
        act = act_ref[...]

        def one(k, carry):
            level = (me_ref[0] ^ (k // share)) * share + lax.rem(k, share)
            c = c_ref[level]
            east = h_ref[level // per]
            east = pltpu.roll(east, width - MAXSUB * lax.rem(level, per), 1)
            both = jnp.where(lane < MAXSUB, east, c)
            moved = [c]
            for j in range(1, MAXSUB):
                moved.append(
                    jnp.where(lane < width - MAXSUB, pltpu.roll(c, width - j, 1), pltpu.roll(both, width - j, 1))
                )
            w = [jnp.ones((rows, width), jnp.float32)]
            for s in range(MAXSUB):
                on = act > s
                rate = [jnp.where(on, x, 0.0) for x in moved[: s + 1]]
                new = [w[0] * (1.0 - rate[0])]
                for q in range(1, s + 1):
                    new.append(w[q] * (1.0 - rate[q]) + w[q - 1] * rate[q - 1])
                new.append(w[s] * rate[s])
                w = new
            for q in range(MAXSUB + 1):
                inner = lane < width - q
                x = jnp.where(inner, w[q], 0.0)
                w_ref[q, k] = x
                if q:
                    x = jnp.where(inner, 0.0, w[q])
                    reach = MAXSUB
                    while reach < width:
                        x = x + pltpu.roll(x, reach, 1)
                        reach *= 2
                    p_ref[q - 1, k] = x
            return carry

        lax.fori_loop(0, levels, one, 0, unroll=4)

    size = levels * rows * width
    return call(
        kernel, [SCALAR, NEAR, NEAR, NEAR] + [ANY] * len(tokens), [me, courant, halo, active, *tokens], [NEAR, NEAR],
        [f32(MAXSUB + 1, levels, rows, width), f32(MAXSUB, levels, rows, width)], size * 300, size * 80, cost=STENCIL_COST,
    )


def beyond(halos, packed, first):
    share, width = halos[0].shape[1], halos[0].shape[3]
    levels, rows = packed.shape[1:3]
    count = len(halos)

    def kernel(*refs):
        hs, p, o = refs[:count], refs[count], refs[-1]
        for r in range(count):
            to, part = slice(r * share, (r + 1) * share), slice((first + r) * share, (first + r + 1) * share)
            high = hs[r].shape[2]
            for g in range(rows // high):
                row = slice(g * high, (g + 1) * high)
                h = hs[r][g]
                total = p[MAXSUB - 1, part, row, :] * h
                for k in range(1, MAXSUB):
                    total = total + p[k - 1, part, row, :] * pltpu.roll(h, MAXSUB - k, 2)
                o[to, row, :] = total

    def block_of(h):
        extra = rows // h.shape[2]
        last = h.shape[0] // extra - 1
        return pl.BlockSpec((extra, share, h.shape[2], width), lambda i: (last, 0, 0, 0))

    size = count * share * rows * width
    return call(
        kernel, [block_of(h) for h in halos] + [pl.BlockSpec(packed.shape, lambda i: (0, 0, 0, 0))],
        list(halos) + [packed], pl.BlockSpec((count * share, rows, width), lambda i: (0, 0, 0)),
        f32(count * share, rows, width), size * 24, size * 40, grid=(1,),
    )


def coefficients(me, courant_lat, mass, entrain, cloud, north, n):
    levels, rows, width = mass.shape
    share = levels // n

    def kernel(me_ref, lat_ref, mass_ref, entrain_ref, cloud_ref, north_ref, rate_ref, inside_ref, detrain_ref):
        total = jnp.zeros((rows, width), jnp.float32)
        base, top = cloud_ref[0], cloud_ref[1]
        for r in range(n):
            for l in range(share):
                level = (me_ref[0] ^ r) * share + l
                inside = jnp.where((level >= base) & (level <= top), 1.0, 0.0)
                air = inside * mass_ref[level]
                total = total + air
                inside_ref[r * share + l] = inside
                detrain_ref[r * share + l] = air
                rate_ref[r * share + l] = lat_ref[level] * north_ref[...]
        factor = entrain_ref[...] / total
        for l in range(levels):
            detrain_ref[l] = detrain_ref[l] * factor

    size = levels * rows * width
    return call(
        kernel, [SCALAR] + [NEAR] * 5, [me, courant_lat, mass, entrain, cloud, north], [NEAR] * 3,
        [f32(levels, rows, width)] * 3, size * 10, size * 20,
    )


def stepped(a, weights):
    axis, width = a.ndim - 1, a.shape[-1]
    total = weights[0] * a
    for k in range(1, MAXSUB + 1):
        total = total + weights[k] * pltpu.roll(a, width - k, axis)
    return total


def added(packed, shift, past, step):
    return jnp.stack([jnp.where(past, pltpu.roll(packed, shift - MAXSUB * m, 1), 0.0) for m in range(step)])


def swept(me, blocks, first, weights, extra, start, moments, rows, step):
    count = len(blocks)
    levels, width = weights.shape[1], weights.shape[3]
    size = extra.shape[0]
    share = size // count

    def kernel(me_ref, *refs):
        a, (w_ref, x_ref, o, e) = refs[:count], refs[count:]
        past = lax.broadcasted_iota(jnp.int32, (HALF, width), 1) >= width - MAXSUB
        shift = width - MAXSUB - MAXSUB * (start + pl.program_id(0) * step)
        for g in range(rows // HALF):
            part = slice(g * HALF, (g + 1) * HALF)
            for r in range(count):
                for l in range(share):
                    k = r * share + l
                    x = stepped(a[r][:, l, part, :], [w_ref[q, first * share + k, part, :] for q in range(MAXSUB + 1)])
                    x = x + added(x_ref[k, part, :], shift, past, step)
                    o[:, k, part, :] = x
                    if g == 0:
                        e[:, k : k + 1, :] = x[:, :1, :]

    in_specs = [pl.BlockSpec((step, share, rows, width), index) for _, index in blocks]
    in_specs += [
        pl.BlockSpec((MAXSUB + 1, levels, rows, width), lambda i, me: (0, 0, 0, 0)),
        pl.BlockSpec((size, rows, width), lambda i, me: (0, 0, 0)),
    ]
    work = moments * size * rows * width
    return prefetched(
        kernel, (moments // step,), in_specs,
        [
            pl.BlockSpec((step, size, rows, width), lambda i, me: (i, 0, 0, 0)),
            pl.BlockSpec((step, size, width), lambda i, me: (i, 0, 0)),
        ],
        [f32(moments, size, rows, width), f32(moments, size, width)],
        [me] + [array for array, _ in blocks] + [weights, extra], work * 25, work * 8,
    )


def prefetched(kernel, grid, in_specs, out_specs, out_shape, operands, flops, moved, aliases=None):
    return pl.pallas_call(
        kernel,
        grid_spec=pltpu.PrefetchScalarGridSpec(num_scalar_prefetch=1, grid=grid, in_specs=in_specs, out_specs=out_specs),
        out_shape=out_shape,
        input_output_aliases=aliases or {},
        compiler_params=pltpu.CompilerParams(vmem_limit_bytes=VMEM_LIMIT),
        cost_estimate=pl.CostEstimate(flops=min(flops, COST), bytes_accessed=min(moved, COST), transcendentals=0),
    )(*operands)


def finish(me, out, first, count, close, low, offset, norths, weights, extra, edges, rate, inside, detrain, entrain, step):
    many = len(norths)
    n = many + 2
    levels, rows, width = rate.shape
    share = levels // n
    moments = close.shape[0]
    base = first // step
    low_base = (first - offset) // step

    def kernel(me_ref, close_ref, low_ref, *refs):
        a = refs[:many]
        w_ref, x_ref, e_close, e_far, rate_ref, inside_ref, detrain_ref, entrain_ref = refs[many : many + 8]
        o = refs[-1]
        top_row = lax.broadcasted_iota(jnp.int32, (step, HALF, width), 1) == HALF - 1
        past = lax.broadcasted_iota(jnp.int32, (HALF, width), 1) >= width - MAXSUB
        groups = (slice(0, HALF), slice(HALF, 2 * HALF))
        shift = width - MAXSUB - MAXSUB * (first + pl.program_id(0) * step)
        sums = [jnp.zeros((step, HALF, width), jnp.float32) for _ in groups]
        for r in range(n):
            owner = (me_ref[0] ^ r) * share
            for l in range(share):
                k = r * share + l
                if r < 2:
                    f = [close_ref[:, k, part, :] for part in groups]
                    edge = e_close[:, k : k + 1, :]
                else:
                    j = k - 2 * share
                    x = stepped(a[r - 2][:, l], [w_ref[q, k] for q in range(MAXSUB + 1)])
                    f = [low_ref[:, j], x + added(x_ref[j], shift, past, step)]
                    edge = e_far[:, j : j + 1, :]
                up = [pltpu.roll(x, HALF - 1, 1) for x in f]
                north = [
                    jnp.where(top_row, up[1], up[0]),
                    jnp.where(top_row, jnp.broadcast_to(edge, (step, HALF, width)), up[1]),
                ]
                for g, part in enumerate(groups):
                    moved = f[g] + rate_ref[k, part, :] * (north[g] - f[g])
                    sums[g] = sums[g] + inside_ref[k, part, :] * moved
                    o[:, owner + l, part, :] = moved
        for r in range(n):
            owner = (me_ref[0] ^ r) * share
            for l in range(share):
                k = r * share + l
                for g, part in enumerate(groups):
                    keep = 1.0 - entrain_ref[part, :] * inside_ref[k, part, :]
                    o[:, owner + l, part, :] = keep * o[:, owner + l, part, :] + detrain_ref[k, part, :] * sums[g]

    full = pl.BlockSpec((levels, rows, width), lambda i, me: (0, 0, 0))
    here = lambda i, me: (i + base, 0, 0, 0)
    in_specs = [
        pl.BlockSpec((step, 2 * share, rows, width), here),
        pl.BlockSpec((step, many * share, HALF, width), lambda i, me: (i + low_base, 0, 0, 0)),
    ]
    in_specs += [pl.BlockSpec((step, share, HALF, width), lambda i, me: (i, 0, 0, 0))] * many
    in_specs += [
        pl.BlockSpec((MAXSUB + 1, levels, HALF, width), lambda i, me: (0, 0, 1, 0)),
        pl.BlockSpec((many * share, HALF, width), lambda i, me: (0, 1, 0)),
        pl.BlockSpec((step, 2 * share, width), lambda i, me: (i + base, 0, 0)),
        pl.BlockSpec((step, many * share, width), lambda i, me: (i + low_base, 0, 0)),
    ]
    in_specs += [full] * 3 + [pl.BlockSpec((rows, width), lambda i, me: (0, 0))]
    operands = [me, close, low] + list(norths) + [weights, extra] + list(edges) + [rate, inside, detrain, entrain]
    aliases = None
    if out is not None:
        aliases = {len(operands): 0}
        in_specs.append(pl.BlockSpec(memory_space=pl.ANY))
        operands.append(out)
    work = count * levels * rows * width
    return prefetched(
        kernel, (count // step,), in_specs, pl.BlockSpec((step, levels, rows, width), here),
        f32(moments, levels, rows, width), operands, work * 30, work * 8, aliases,
    )


def body(adj_in, courant_lon, courant_lat, mass, entrain, cloud, substeps):
    n = lax.axis_size("lon")
    moments, share, rows, _ = adj_in.shape
    width = courant_lon.shape[2]
    me = lax.axis_index("lon").astype(jnp.int32)[None]
    partners = list(range(2, n))

    def exchanged(blocks):
        return [swapped(b, r) for b, r in zip(blocks, partners)]

    south, upper = slice(0, HALF), slice(HALF, 2 * HALF)
    rates = packed_rates(me, courant_lon)
    firsts = taken(me, adj_in, width, [(r, 0, FIRST, south) for r in partners], rates)
    rates = sent_west(rates)
    firsts = exchanged([held_for(b, rates) for b in firsts])
    own_halo, near, *rests = prepared(me, adj_in, width, n, firsts[0])
    near = swapped(near, 1)
    rests = exchanged(rests)

    active = jnp.broadcast_to(substeps[:, None], (rows, width))
    latitude = lax.axis_index("lat") * rows + jnp.arange(rows, dtype=jnp.int32)
    has_north = (latitude < rows * lax.axis_size("lat") - 1).astype(jnp.float32)
    has_north = jnp.broadcast_to(has_north[:, None], (rows, width))
    rate, inside, detrain = coefficients(me, courant_lat, mass, entrain, cloud, has_north, n)
    weights, packed = stencil(me, courant_lon, rates, active, n, rate, firsts[-1])

    whole = lambda i, me: (i, 0, 0, 0)
    extra = beyond([own_halo, near], packed, 0)
    blocks = [(adj_in, lambda i, me: (i, 0, 0, me[0])), (near, whole)]
    close, edge_close = swept(me, blocks, 0, weights, extra, 0, moments, rows, 4)
    edge_close = sent_south(edge_close)
    extra = beyond(rests, packed, 2)
    lows = []
    for start, size, arrays in ((0, FIRST, firsts), (FIRST, moments - FIRST, rests)):
        low, edge = swept(me, [(array, whole) for array in arrays], 2, weights, extra, start, size, HALF, 4)
        lows.append((low, start, sent_south(edge)))

    parts, start = [], 0
    for size in NORTH_CHUNKS:
        parts += [(r, start, size, upper) for r in partners]
        start += size
    sent = taken(me, adj_in, width, parts, firsts[-1])
    out, start = None, 0
    for i, size in enumerate(NORTH_CHUNKS):
        blocks = exchanged(sent[i * (n - 2) : (i + 1) * (n - 2)])
        low, offset, edge = lows[0] if start < FIRST else lows[1]
        out = finish(
            me, out, start, size, close, low, offset, blocks, weights, extra, [edge_close, edge],
            rate, inside, detrain, entrain, 2,
        )
        start += size
    return out


def solution(mesh):
    return jax.shard_map(
        body,
        mesh=mesh,
        in_specs=(
            P(None, "lon", "lat", None),
            P(None, "lat", "lon"),
            P(None, "lat", "lon"),
            P(None, "lat", "lon"),
            P("lat", "lon"),
            P(None, "lat", "lon"),
            P("lat"),
        ),
        out_specs=P(None, None, "lat", "lon"),
        check_vma=False,
    )
```

time: 563 us -> 67.6 us (0.12)
  local copies, waits for them, and re-layouts: 413 us -> 4.01 us
  other arithmetic: 85.1 us -> 0.01 us
  waiting for transfers between devices: 46.1 us -> 15.8 us
  Pallas kernels: 0 us -> 29.4 us
    another operation x16 -> x0, local copies, waits for them, and re-layouts: 188 us -> none
    unnamed x19 -> x26, local copies, waits for them, and re-layouts: 81.3 us -> 3.86 us
    add x9 -> x0, other arithmetic: 66.5 us -> none  [the longest x8 63.3 us: sweep_once(): return state + active * courant[None] * (neighbour(state) - state)]
    slice x18 -> x0, local copies, waits for them, and re-layouts: 53.5 us -> none  [the longest x8 42.4 us: east_neighbour(): return jnp.concatenate([field[:, :, :, 1:], edge], axis=3)]
    all_to_all x1 -> x0, waiting for transfers between devices: 46 us -> none  [to_columns(): return lax.all_to_all(field, 'lon', split_axis=3, concat_axis=1, tiled=True)]
    while x4 -> x0, local copies, waits for them, and re-layouts: 36 us -> none  [sweep_all(): return lax.fori_loop(0, MAXSUB, sweep_once, field)]
    pallas_call x0 -> x16, Pallas kernels: none -> 29.4 us  [the longest x6 15.3 us: prefetched(): pl.pallas_call(kernel, grid_spec=pltpu.PrefetchScalarGridSpec(num_scalar_...]
    all_to_all x3 -> x0, local copies, waits for them, and re-layouts: 25.8 us -> none  [to_columns(): return lax.all_to_all(field, 'lon', split_axis=3, concat_axis=1, tiled=True)]
  transfers between devices with their start and end apart: 10 -> 15, of which waited for: 1 -> 4; matrix products, arithmetic and copies ran while one was open for 29% -> 0% of each run, Pallas kernels for 0% -> 35%
where the time goes in v2:
time: 67.6 us; the launch traced here: 66.4 us
  Pallas kernels  29.4 us (43%)
  starting transfers between devices  16.9 us (25%)
  waiting for transfers between devices  15.8 us (23%)
  local copies, waits for them, and re-layouts  4.01 us (6%)
    pallas_call x6, Pallas kernels, prefetched(): pl.pallas_call(kernel, grid_spec=pltpu.PrefetchScalarGridSpec(num_scalar_...  15.3 us
    pallas_call x10, Pallas kernels, call(): pl.pallas_call(kernel, in_specs=in_specs, out_specs=out_specs, out_shape=...  14.1 us
    ppermute x11, waiting for transfers between devices, swapped(): return lax.ppermute(block, 'lon', [(i, i ^ r) for i in range(n)])  13.2 us
    ppermute x11, starting transfers between devices, swapped(): return lax.ppermute(block, 'lon', [(i, i ^ r) for i in range(n)])  10.2 us
    ppermute x3, starting transfers between devices, sent_south(): return lax.ppermute(block, 'lat', [(i + 1, i) for i in range(n - 1)])  5.98 us
    unnamed x26, local copies, waits for them, and re-layouts  3.86 us
    ppermute x1, waiting for transfers between devices, sent_west(): return lax.ppermute(block, 'lon', [(i, (i - 1) % n) for i in range(n)])  1.46 us
  transfers between devices with their start and end apart: 15, of which 4 were waited for; matrix products, arithmetic and copies ran while one was open for 0% of the time, Pallas kernels for 35%

profile of v2, /device:TPU:5, one launch (start us, length us, event | category | flops | bytes accessed | tf_op | source)
XLA Modules:
  0.0 66.4 jit_solution(11543646073550407173)
XLA Ops:
  0.0 0.9 %copy-done.1 = f32[32,16,128]{2,1,0:T(8,128)S(1)} copy-done((f32[32,16,128]{2,1,0:T(8,128)S(1)}, f32[32,16,128]{2,1,0:T(8,128)}, u32[]{:S(2)}) %copy-start.1) | copy-done | bytes 262168
  1.8 1.0 %shard_map.74 = (f32[8,8,8,128]{3,2,1,0:T(8,128)S(1)}, f32[8,8,8,128]{3,2,1,0:T(8,128)S(1)}) custom-call(s32[1]{0:T(128)} %bitcast.me_ref, f32[16,8,16,512]{3,2,1,0:T(8,128)} %a.5, f32[2,16,128]{2,1,0:T(8,128)S(1)} %shard_map.73.refs_0_), custom_call_target="tpu_custom_call" | custom-call | flops 1024 | bytes 1024 | tf_op jit(solution)/shard_map/pallas_call | solution.py:46
  2.9 1.5 %collective-permute-done.t.h_ref = f32[2,16,128]{2,1,0:T(8,128)S(1)} collective-permute-done((f32[2,16,128]{2,1,0:T(8,128)S(1)}, f32[2,16,128]{2,1,0:T(8,128)S(1)}, u32[]{:S(2)}, u32[]{:S(2)}) %collective-permute-start) | collective-permute-done | bytes 16416 | tf_op jit(solution)/shard_map/ppermute | solution.py:27
  4.3 1.2 %collective-permute-start.1 = (f32[8,8,8,128]{3,2,1,0:T(8,128)S(1)}, f32[8,8,8,128]{3,2,1,0:T(8,128)S(1)}, u32[]{:S(2)}, u32[]{:S(2)}) collective-permute-start(f32[8,8,8,128]{3,2,1,0:T(8,128)S(1)} %shard_map.75), channel_id=1, source_target_pairs={{0,2},{1,3},{2,0},{3,1},{4,6},{5,7},{6,4},{7,5},{8,10},{9,11},{10,... | collective-permute-start | bytes 786440 | tf_op jit(solution)/shard_map/ppermute | solution.py:22
  5.5 6.8 %collective-permute-done.1.refs_0_ = f32[8,8,8,128]{3,2,1,0:T(8,128)S(1)} collective-permute-done((f32[8,8,8,128]{3,2,1,0:T(8,128)S(1)}, f32[8,8,8,128]{3,2,1,0:T(8,128)S(1)}, u32[]{:S(2)}, u32[]{:S(2)}) %collective-permute-start.1) | collective-permute-done | bytes 262176 | tf_op jit(solution)/shard_map/ppermute | solution.py:22
  12.3 5.1 %shard_map.76 = (f32[1,8,16,128]{3,2,1,0:T(8,128)S(1)}, f32[17,8,16,128]{3,2,1,0:T(8,128)}, f32[10,8,8,128]{3,2,1,0:T(8,128)}, f32[10,8,8,128]{3,2,1,0:T(8,128)}) custom-call(s32[1]{0:T(128)} %bitcast.me_ref, f32[16,8,16,512]{3,2,1,0:T(8,128)} %a.5, f32[8,8,8,128]{3,2,1,0:T(8,128)S(1)} %collective-permute-done.1.refs_0_), custom_call_target="tpu_custom_call" | custom-call | flops 1024 | bytes 1024 | tf_op jit(solution)/shard_map/pallas_call | solution.py:46
  18.6 1.2 %collective-permute-start.4 = (f32[10,8,8,128]{3,2,1,0:T(8,128)}, f32[10,8,8,128]{3,2,1,0:T(8,128)S(1)}, u32[]{:S(2)}, u32[]{:S(2)}) collective-permute-start(f32[10,8,8,128]{3,2,1,0:T(8,128)} %get-tuple-element.36), channel_id=1, source_target_pairs={{0,2},{1,3},{2,0},{3,1},{4,6},{5,7},{6,4},{7,5},{8,10},{9,11},{10,... | collective-permute-start | bytes 983048 | tf_op jit(solution)/shard_map/ppermute | solution.py:22
  20.5 6.3 %collective-permute-done.3.refs_1_.refs_0_ = f32[8,8,8,128]{3,2,1,0:T(8,128)S(1)} collective-permute-done((f32[8,8,8,128]{3,2,1,0:T(8,128)S(1)}, f32[8,8,8,128]{3,2,1,0:T(8,128)S(1)}, u32[]{:S(2)}, u32[]{:S(2)}) %collective-permute-start.3) | collective-permute-done | bytes 262176 | tf_op jit(solution)/shard_map/ppermute | solution.py:22
  26.8 2.0 %shard_map.84 = (f32[8,8,8,128]{3,2,1,0:T(8,128)}, f32[8,8,8,128]{3,2,1,0:T(8,128)}, f32[6,8,8,128]{3,2,1,0:T(8,128)S(1)}, f32[6,8,8,128]{3,2,1,0:T(8,128)S(1)},...) custom-call(s32[1]{0:T(128)} %bitcast.me_ref, f32[16,8,16,512]{3,2,1,0:T(8,128)} %a.5, ...), custom_call_target="tpu_custom_call" | custom-call | flops 1024 | bytes 1024 | tf_op jit(solution)/shard_map/pallas_call | solution.py:46
  30.9 1.2 %collective-permute-start.13 = (f32[8,8,8,128]{3,2,1,0:T(8,128)}, f32[8,8,8,128]{3,2,1,0:T(8,128)S(1)}, u32[]{:S(2)}, u32[]{:S(2)}) collective-permute-start(f32[8,8,8,128]{3,2,1,0:T(8,128)} %get-tuple-element.49), channel_id=1, source_target_pairs={{0,3},{1,2},{2,1},{3,0},{4,7},{5,6},{6,5},{7,4},{8,11},{9,10},{10,... | collective-permute-start | bytes 786440 | tf_op jit(solution)/shard_map/ppermute | solution.py:22
  32.2 0.9 %copy-done.4 = f32[32,16,128]{2,1,0:T(8,128)S(1)} copy-done((f32[32,16,128]{2,1,0:T(8,128)S(1)}, f32[32,16,128]{2,1,0:T(8,128)}, u32[]{:S(2)}) %copy-start.4) | copy-done | bytes 262168
  33.4 5.1 %shard_map.79 = (f32[9,32,16,128]{3,2,1,0:T(8,128)S(1)}, f32[8,32,16,128]{3,2,1,0:T(8,128)S(1)}) custom-call(s32[1]{0:T(128)} %bitcast.me_ref, f32[32,16,128]{2,1,0:T(8,128)S(1)} %copy-done.2, f32[2,16,128]{2,1,0:T(8,128)S(1)} %collective-permute-done.t.h_ref, s32[16,128]{1,0:T(8,128)S(1)} %broadcast_in_dim.7.act_ref, ...), custom_call_target="tpu_custom_call" | custom-call | flops 19660800 | bytes 200000000 | tf_op jit(solution)/shard_map/pallas_call | solution.py:46
  39.3 1.8 %collective-permute-start.11 = (f32[6,8,8,128]{3,2,1,0:T(8,128)S(1)}, f32[6,8,8,128]{3,2,1,0:T(8,128)S(1)}, u32[]{:S(2)}, u32[]{:S(2)}) collective-permute-start(f32[6,8,8,128]{3,2,1,0:T(8,128)S(1)} %copy-done.8), channel_id=1, source_target_pairs={{0,3},{1,2},{2,1},{3,0},{4,7},{5,6},{6,5},{7,4},{8,11},{9,10},{10,... | collective-permute-start | bytes 589832 | tf_op jit(solution)/shard_map/ppermute | solution.py:22
  41.1 5.3 %shard_map.81 = (f32[16,16,16,128]{3,2,1,0:T(8,128)S(1)}, f32[16,16,128]{2,1,0:T(8,128)S(1)}) custom-call(s32[1]{0:T(128)} %bitcast.me_ref, f32[16,8,16,512]{3,2,1,0:T(8,128)S(1)} %copy-done, f32[17,8,16,128]{3,2,1,0:T(8,128)S(1)} %collective-permute-done.2.refs_1_, f32[9,32,16,128]{3,2,1,0:T(8,128)S(1)} %get-tuple-element.32.refs_2_, ...), custom_call_target="tpu_custom_call" | custom-call | flops 1024 | bytes 1024 | tf_op jit(solution)/shard_map/pallas_call | solution.py:324
  46.4 2.1 %collective-permute-start.8 = (f32[16,16,128]{2,1,0:T(8,128)S(1)}, f32[16,16,128]{2,1,0:T(8,128)S(1)}, u32[]{:S(2)}, u32[]{:S(2)}) collective-permute-start(f32[16,16,128]{2,1,0:T(8,128)S(1)} %get-tuple-element.41), channel_id=1, source_target_pairs={{4,0},{8,4},{12,8},{16,12},{20,16},{24,20},{28,24},{5,1},{9,5},{13... | collective-permute-start | bytes 393224 | tf_op jit(solution)/shard_map/ppermute | solution.py:32
  48.9 1.5 %shard_map.85 = (f32[8,16,8,128]{3,2,1,0:T(8,128)S(1)}, f32[8,16,128]{2,1,0:T(8,128)S(1)}) custom-call(s32[1]{0:T(128)} %bitcast.me_ref, f32[8,8,8,128]{3,2,1,0:T(8,128)S(1)} %collective-permute-done.1.refs_0_, f32[8,8,8,128]{3,2,1,0:T(8,128)S(1)} %collective-permute-done.3.refs_1_.refs_0_, f32[9,32,16,128]{3,2,1,0:T(8,128)S(1)} %get-tuple-element.32.refs_2_, ...), custom_call_target="tpu_custom_call" | custom-call | flops 1024 | bytes 1024 | tf_op jit(solution)/shard_map/pallas_call | solution.py:324
  50.4 1.9 %collective-permute-start.14 = (f32[8,16,128]{2,1,0:T(8,128)S(1)}, f32[8,16,128]{2,1,0:T(8,128)S(1)}, u32[]{:S(2)}, u32[]{:S(2)}) collective-permute-start(f32[8,16,128]{2,1,0:T(8,128)S(1)} %get-tuple-element.50), channel_id=1, source_target_pairs={{4,0},{8,4},{12,8},{16,12},{20,16},{24,20},{28,24},{5,1},{9,5},{13... | collective-permute-start | bytes 196616 | tf_op jit(solution)/shard_map/ppermute | solution.py:32
  52.3 1.5 %shard_map.83 = (f32[8,16,8,128]{3,2,1,0:T(8,128)S(1)}, f32[8,16,128]{2,1,0:T(8,128)S(1)}) custom-call(s32[1]{0:T(128)} %bitcast.me_ref, f32[10,8,8,128]{3,2,1,0:T(8,128)S(1)} %collective-permute-done.4.refs_0_, f32[10,8,8,128]{3,2,1,0:T(8,128)S(1)} %collective-permute-done.5.refs_1_, f32[9,32,16,128]{3,2,1,0:T(8,128)S(1)} %get-tuple-element.32.refs_2_, ...), custom_call_target="tpu_custom_call" | custom-call | flops 1024 | bytes 1024 | tf_op jit(solution)/shard_map/pallas_call | solution.py:324
  53.8 1.9 %collective-permute-start.9 = (f32[8,16,128]{2,1,0:T(8,128)S(1)}, f32[8,16,128]{2,1,0:T(8,128)S(1)}, u32[]{:S(2)}, u32[]{:S(2)}) collective-permute-start(f32[8,16,128]{2,1,0:T(8,128)S(1)} %get-tuple-element.42), channel_id=1, source_target_pairs={{4,0},{8,4},{12,8},{16,12},{20,16},{24,20},{28,24},{5,1},{9,5},{13... | collective-permute-start | bytes 196616 | tf_op jit(solution)/shard_map/ppermute | solution.py:32
  55.7 1.2 %collective-permute-done.14.refs_5_ = f32[8,16,128]{2,1,0:T(8,128)S(1)} collective-permute-done((f32[8,16,128]{2,1,0:T(8,128)S(1)}, f32[8,16,128]{2,1,0:T(8,128)S(1)}, u32[]{:S(2)}, u32[]{:S(2)}) %collective-permute-start.14) | collective-permute-done | bytes 65568 | tf_op jit(solution)/shard_map/ppermute | solution.py:32
  56.9 2.4 %collective-permute-start.7 = (f32[2,8,8,128]{3,2,1,0:T(8,128)S(1)}, f32[2,8,8,128]{3,2,1,0:T(8,128)S(1)}, u32[]{:S(2)}, u32[]{:S(2)}) collective-permute-start(f32[2,8,8,128]{3,2,1,0:T(8,128)S(1)} %get-tuple-element.40), channel_id=1, source_target_pairs={{0,3},{1,2},{2,1},{3,0},{4,7},{5,6},{6,5},{7,4},{8,11},{9,10},{10,... | collective-permute-start | bytes 196616 | tf_op jit(solution)/shard_map/ppermute | solution.py:22
  59.3 3.1 %shard_map.86.refs_10_ = f32[16,32,16,128]{3,2,1,0:T(8,128)} custom-call(s32[1]{0:T(128)} %bitcast.me_ref, f32[16,16,16,128]{3,2,1,0:T(8,128)S(1)} %get-tuple-element.35.close_ref, f32[8,16,8,128]{3,2,1,0:T(8,128)S(1)} %get-tuple-element.47.low_ref, f32[8,8,8,128]{3,2,1,0:T(8,128)S(1)} %collective-permute-done.12.refs_0_, ...), custom_call_target="tpu_custom_call" | custom-call | flops 1024 | bytes 1024 | tf_op jit(solution)/shard_map/pallas_call | solution.py:324
  62.4 2.7 %shard_map.87.refs_10_ = f32[16,32,16,128]{3,2,1,0:T(8,128)} custom-call(s32[1]{0:T(128)} %bitcast.me_ref, f32[16,16,16,128]{3,2,1,0:T(8,128)S(1)} %get-tuple-element.35.close_ref, f32[8,16,8,128]{3,2,1,0:T(8,128)S(1)} %get-tuple-element.38.low_ref, f32[6,8,8,128]{3,2,1,0:T(8,128)S(1)} %collective-permute-done.10.refs_0_, ...), custom_call_target="tpu_custom_call", output_to_operand_aliasing={{}: (13, {})} | custom-call | flops 1024 | bytes 1024 | tf_op jit(solution)/shard_map/pallas_call | solution.py:324
  65.1 1.3 %shard_map.88 = f32[16,32,16,128]{3,2,1,0:T(8,128)} custom-call(s32[1]{0:T(128)} %bitcast.me_ref, f32[16,16,16,128]{3,2,1,0:T(8,128)S(1)} %get-tuple-element.35.close_ref, f32[8,16,8,128]{3,2,1,0:T(8,128)S(1)} %get-tuple-element.38.low_ref, f32[2,8,8,128]{3,2,1,0:T(8,128)S(1)} %collective-permute-done.6.refs_0_, ...), custom_call_target="tpu_custom_call", output_to_operand_aliasing={{}: (13, {})} | custom-call | flops 1024 | bytes 1024 | tf_op jit(solution)/shard_map/pallas_call | solution.py:324
  (51 shorter events, 6.2 us)
Async XLA Ops:
  1.1 3.2 %collective-permute-start = (f32[2,16,128]{2,1,0:T(8,128)S(1)}, f32[2,16,128]{2,1,0:T(8,128)S(1)}, u32[]{:S(2)}, u32[]{:S(2)}) collective-permute-start(f32[2,16,128]{2,1,0:T(8,128)S(1)} %shard_map.73.refs_0_), channel_id=1, source_target_pairs={{0,3},{1,0},{2,1},{3,2},{4,7},{5,4},{6,5},{7,6},{8,11},{9,8},{10,9... | collective-permute-start | bytes 49160 | tf_op jit(solution)/shard_map/ppermute | solution.py:27
  4.3 8.0 %collective-permute-start.1 = (f32[8,8,8,128]{3,2,1,0:T(8,128)S(1)}, f32[8,8,8,128]{3,2,1,0:T(8,128)S(1)}, u32[]{:S(2)}, u32[]{:S(2)}) collective-permute-start(f32[8,8,8,128]{3,2,1,0:T(8,128)S(1)} %shard_map.75), channel_id=1, source_target_pairs={{0,2},{1,3},{2,0},{3,1},{4,6},{5,7},{6,4},{7,5},{8,10},{9,11},{10,... | collective-permute-start | bytes 786440 | tf_op jit(solution)/shard_map/ppermute | solution.py:22
  17.5 21.0 %collective-permute-start.2 = (f32[17,8,16,128]{3,2,1,0:T(8,128)}, f32[17,8,16,128]{3,2,1,0:T(8,128)S(1)}, u32[]{:S(2)}, u32[]{:S(2)}) collective-permute-start(f32[17,8,16,128]{3,2,1,0:T(8,128)} %get-tuple-element.29), channel_id=1, source_target_pairs={{0,1},{1,0},{2,3},{3,2},{4,5},{5,4},{6,7},{7,6},{8,9},{9,8},{10,11... | collective-permute-start | bytes 3342344 | tf_op jit(solution)/shard_map/ppermute | solution.py:22
  18.2 14.0 %copy-start.3 = (f32[32,16,128]{2,1,0:T(8,128)S(1)}, f32[32,16,128]{2,1,0:T(8,128)}, u32[]{:S(2)}) copy-start(f32[32,16,128]{2,1,0:T(8,128)} %lat_ref.1) | copy-start | bytes 786436
  18.2 14.0 %copy-start.5 = (f32[16,128]{1,0:T(8,128)S(1)}, f32[16,128]{1,0:T(8,128)}, u32[]{:S(2)}) copy-start(f32[16,128]{1,0:T(8,128)} %refs_9_.5) | copy-start | bytes 24580
  18.2 14.0 %copy-start.6 = (s32[2,16,128]{2,1,0:T(8,128)S(1)}, s32[2,16,128]{2,1,0:T(8,128)}, u32[]{:S(2)}) copy-start(s32[2,16,128]{2,1,0:T(8,128)} %cloud_ref.1) | copy-start | bytes 49156
  18.2 8.5 %collective-permute-start.3 = (f32[8,8,8,128]{3,2,1,0:T(8,128)S(1)}, f32[8,8,8,128]{3,2,1,0:T(8,128)S(1)}, u32[]{:S(2)}, u32[]{:S(2)}) collective-permute-start(f32[8,8,8,128]{3,2,1,0:T(8,128)S(1)} %shard_map.78), channel_id=1, source_target_pairs={{0,3},{1,2},{2,1},{3,0},{4,7},{5,6},{6,5},{7,4},{8,11},{9,10},{10,... | collective-permute-start | bytes 786440 | tf_op jit(solution)/shard_map/ppermute | solution.py:22
  18.6 20.7 %collective-permute-start.4 = (f32[10,8,8,128]{3,2,1,0:T(8,128)}, f32[10,8,8,128]{3,2,1,0:T(8,128)S(1)}, u32[]{:S(2)}, u32[]{:S(2)}) collective-permute-start(f32[10,8,8,128]{3,2,1,0:T(8,128)} %get-tuple-element.36), channel_id=1, source_target_pairs={{0,2},{1,3},{2,0},{3,1},{4,6},{5,7},{6,4},{7,5},{8,10},{9,11},{10,... | collective-permute-start | bytes 983048 | tf_op jit(solution)/shard_map/ppermute | solution.py:22
  19.7 13.5 %copy-start.12 = (s32[16]{0:T(128)S(1)}, s32[16]{0:T(128)}, u32[]{:S(2)}) copy-start(s32[16]{0:T(128)} %param.13) | copy-start | bytes 196
  19.7 13.6 %copy-start.2 = (f32[32,16,128]{2,1,0:T(8,128)S(1)}, f32[32,16,128]{2,1,0:T(8,128)}, u32[]{:S(2)}) copy-start(f32[32,16,128]{2,1,0:T(8,128)} %c_ref.1) | copy-start | bytes 786436
  19.7 26.7 %collective-permute-start.5 = (f32[10,8,8,128]{3,2,1,0:T(8,128)}, f32[10,8,8,128]{3,2,1,0:T(8,128)S(1)}, u32[]{:S(2)}, u32[]{:S(2)}) collective-permute-start(f32[10,8,8,128]{3,2,1,0:T(8,128)} %get-tuple-element.37), channel_id=1, source_target_pairs={{0,3},{1,2},{2,1},{3,0},{4,7},{5,6},{6,5},{7,4},{8,11},{9,10},{10,... | collective-permute-start | bytes 983048 | tf_op jit(solution)/shard_map/ppermute | solution.py:22
  30.8 19.6 %collective-permute-start.12 = (f32[8,8,8,128]{3,2,1,0:T(8,128)}, f32[8,8,8,128]{3,2,1,0:T(8,128)S(1)}, u32[]{:S(2)}, u32[]{:S(2)}) collective-permute-start(f32[8,8,8,128]{3,2,1,0:T(8,128)} %get-tuple-element.48), channel_id=1, source_target_pairs={{0,2},{1,3},{2,0},{3,1},{4,6},{5,7},{6,4},{7,5},{8,10},{9,11},{10,... | collective-permute-start | bytes 786440 | tf_op jit(solution)/shard_map/ppermute | solution.py:22
  30.9 22.8 %collective-permute-start.13 = (f32[8,8,8,128]{3,2,1,0:T(8,128)}, f32[8,8,8,128]{3,2,1,0:T(8,128)S(1)}, u32[]{:S(2)}, u32[]{:S(2)}) collective-permute-start(f32[8,8,8,128]{3,2,1,0:T(8,128)} %get-tuple-element.49), channel_id=1, source_target_pairs={{0,3},{1,2},{2,1},{3,0},{4,7},{5,6},{6,5},{7,4},{8,11},{9,10},{10,... | collective-permute-start | bytes 786440 | tf_op jit(solution)/shard_map/ppermute | solution.py:22
  32.2 1.0 %copy-start.4 = (f32[32,16,128]{2,1,0:T(8,128)S(1)}, f32[32,16,128]{2,1,0:T(8,128)}, u32[]{:S(2)}) copy-start(f32[32,16,128]{2,1,0:T(8,128)} %mass_ref.1) | copy-start | bytes 786436
  33.2 6.1 %copy-start.8 = (f32[6,8,8,128]{3,2,1,0:T(8,128)S(1)}, f32[6,8,8,128]{3,2,1,0:T(8,128)}, u32[]{:S(2)}) copy-start(f32[6,8,8,128]{3,2,1,0:T(8,128)} %copy-done.7) | copy-start | bytes 589828
  33.2 7.9 %copy-start = (f32[16,8,16,512]{3,2,1,0:T(8,128)S(1)}, f32[16,8,16,512]{3,2,1,0:T(8,128)}, u32[]{:S(2)}) copy-start(f32[16,8,16,512]{3,2,1,0:T(8,128)} %a.5) | copy-start | bytes 12582916
  38.5 24.0 %collective-permute-start.10 = (f32[6,8,8,128]{3,2,1,0:T(8,128)}, f32[6,8,8,128]{3,2,1,0:T(8,128)S(1)}, u32[]{:S(2)}, u32[]{:S(2)}) collective-permute-start(f32[6,8,8,128]{3,2,1,0:T(8,128)} %copy-done.9), channel_id=1, source_target_pairs={{0,2},{1,3},{2,0},{3,1},{4,6},{5,7},{6,4},{7,5},{8,10},{9,11},{10,... | collective-permute-start | bytes 589832 | tf_op jit(solution)/shard_map/ppermute | solution.py:22
  39.3 23.2 %collective-permute-start.11 = (f32[6,8,8,128]{3,2,1,0:T(8,128)S(1)}, f32[6,8,8,128]{3,2,1,0:T(8,128)S(1)}, u32[]{:S(2)}, u32[]{:S(2)}) collective-permute-start(f32[6,8,8,128]{3,2,1,0:T(8,128)S(1)} %copy-done.8), channel_id=1, source_target_pairs={{0,3},{1,2},{2,1},{3,0},{4,7},{5,6},{6,5},{7,4},{8,11},{9,10},{10,... | collective-permute-start | bytes 589832 | tf_op jit(solution)/shard_map/ppermute | solution.py:22
  46.4 10.4 %collective-permute-start.8 = (f32[16,16,128]{2,1,0:T(8,128)S(1)}, f32[16,16,128]{2,1,0:T(8,128)S(1)}, u32[]{:S(2)}, u32[]{:S(2)}) collective-permute-start(f32[16,16,128]{2,1,0:T(8,128)S(1)} %get-tuple-element.41), channel_id=1, source_target_pairs={{4,0},{8,4},{12,8},{16,12},{20,16},{24,20},{28,24},{5,1},{9,5},{13... | collective-permute-start | bytes 393224 | tf_op jit(solution)/shard_map/ppermute | solution.py:32
  48.9 8.0 %copy-start.11 = (f32[2,8,8,128]{3,2,1,0:T(8,128)S(1)}, f32[2,8,8,128]{3,2,1,0:T(8,128)}, u32[]{:S(2)}) copy-start(f32[2,8,8,128]{3,2,1,0:T(8,128)} %copy-done.10) | copy-start | bytes 196612
  50.4 6.5 %collective-permute-start.14 = (f32[8,16,128]{2,1,0:T(8,128)S(1)}, f32[8,16,128]{2,1,0:T(8,128)S(1)}, u32[]{:S(2)}, u32[]{:S(2)}) collective-permute-start(f32[8,16,128]{2,1,0:T(8,128)S(1)} %get-tuple-element.50), channel_id=1, source_target_pairs={{4,0},{8,4},{12,8},{16,12},{20,16},{24,20},{28,24},{5,1},{9,5},{13... | collective-permute-start | bytes 196616 | tf_op jit(solution)/shard_map/ppermute | solution.py:32
  53.8 8.7 %collective-permute-start.9 = (f32[8,16,128]{2,1,0:T(8,128)S(1)}, f32[8,16,128]{2,1,0:T(8,128)S(1)}, u32[]{:S(2)}, u32[]{:S(2)}) collective-permute-start(f32[8,16,128]{2,1,0:T(8,128)S(1)} %get-tuple-element.42), channel_id=1, source_target_pairs={{4,0},{8,4},{12,8},{16,12},{20,16},{24,20},{28,24},{5,1},{9,5},{13... | collective-permute-start | bytes 196616 | tf_op jit(solution)/shard_map/ppermute | solution.py:32
  56.9 8.3 %collective-permute-start.6 = (f32[2,8,8,128]{3,2,1,0:T(8,128)S(1)}, f32[2,8,8,128]{3,2,1,0:T(8,128)S(1)}, u32[]{:S(2)}, u32[]{:S(2)}) collective-permute-start(f32[2,8,8,128]{3,2,1,0:T(8,128)S(1)} %copy-done.11), channel_id=1, source_target_pairs={{0,2},{1,3},{2,0},{3,1},{4,6},{5,7},{6,4},{7,5},{8,10},{9,11},{10,... | collective-permute-start | bytes 196616 | tf_op jit(solution)/shard_map/ppermute | solution.py:22
  56.9 8.2 %collective-permute-start.7 = (f32[2,8,8,128]{3,2,1,0:T(8,128)S(1)}, f32[2,8,8,128]{3,2,1,0:T(8,128)S(1)}, u32[]{:S(2)}, u32[]{:S(2)}) collective-permute-start(f32[2,8,8,128]{3,2,1,0:T(8,128)S(1)} %get-tuple-element.40), channel_id=1, source_target_pairs={{0,3},{1,2},{2,1},{3,0},{4,7},{5,6},{6,5},{7,4},{8,11},{9,10},{10,... | collective-permute-start | bytes 196616 | tf_op jit(solution)/shard_map/ppermute | solution.py:22
  (4 other events, 2.9 us)

commit v3 on v2

--- a/solution.py
+++ b/solution.py
@@ -11,10 +11,8 @@
 HALF = 8
 VMEM_LIMIT = 12 * 1024 * 1024
 COST = 1024
-STENCIL_COST = 2 * 10**8
-FIRST = 8
 VMEM_WIDE = 50 * 1024 * 1024
-NORTH_CHUNKS = (8, 6, 2)
+NORTH_CHUNKS = (10, 4, 2)
 
 
 def swapped(block, r):
@@ -42,7 +40,7 @@
 ANY = pl.BlockSpec(memory_space=pl.ANY)
 
 
-def call(kernel, in_specs, operands, out_specs, out_shape, flops, moved, aliases=None, scratch=(), limit=VMEM_LIMIT, grid=(), cost=None):
+def call(kernel, in_specs, operands, out_specs, out_shape, flops, moved, aliases=None, scratch=(), limit=VMEM_LIMIT, grid=()):
     return pl.pallas_call(
         kernel,
         in_specs=in_specs,
@@ -52,7 +50,7 @@
         scratch_shapes=list(scratch),
         input_output_aliases=aliases or {},
         compiler_params=pltpu.CompilerParams(vmem_limit_bytes=limit),
-        cost_estimate=pl.CostEstimate(flops=min(flops, cost or COST), bytes_accessed=cost or min(moved, COST), transcendentals=0),
+        cost_estimate=pl.CostEstimate(flops=min(flops, COST), bytes_accessed=min(moved, COST), transcendentals=0),
     )(*operands)
 
 
@@ -66,22 +64,6 @@
         pass
 
     return call(kernel, [ANY, ANY], [block, token], ANY, f32(*block.shape), 0, 0, {0: 0})
-
-
-def packed_rates(me, courant):
-    levels, rows, width = courant.shape
-    per = width // MAXSUB
-
-    def kernel(c, o):
-        lane = lax.broadcasted_iota(jnp.int32, (rows, width), 1)
-        for b in range(levels // per):
-            total = jnp.where(lane < MAXSUB, c[b * per], 0.0)
-            for l in range(1, per):
-                total = total + pltpu.roll(jnp.where(lane < MAXSUB, c[b * per + l], 0.0), MAXSUB * l, 1)
-            o[b] = total
-
-    size = levels * rows * width
-    return call(kernel, [NEAR], [courant], NEAR, f32(levels // per, rows, width), size * 3, size * 4)
 
 
 def taken(me, adj, width, parts, *tokens):
@@ -105,68 +87,79 @@
     )
 
 
-def prepared(me, adj, width, n, *tokens):
+def packed_rates(courant, token):
+    levels, rows, width = courant.shape
+    per = width // MAXSUB
+
+    def kernel(c, _, o):
+        lane = lax.broadcasted_iota(jnp.int32, (rows, width), 1)
+        for b in range(levels // per):
+            total = jnp.where(lane < MAXSUB, c[b * per], 0.0)
+            for l in range(1, per):
+                total = total + pltpu.roll(jnp.where(lane < MAXSUB, c[b * per + l], 0.0), MAXSUB * l, 1)
+            o[b] = total
+
+    return call(kernel, [NEAR, ANY], [courant, token], NEAR, f32(levels // per, rows, width), 1024, 1024)
+
+
+def prepared(me, adj, width, n):
     moments, share, rows, _ = adj.shape
     step = 4
     many = n - 2
-    extra = rows // HALF
-    rest = moments - FIRST
-
-    def kernel(me_ref, a, *refs):
-        halo, near, *refs = refs[len(tokens) :]
-        fars, (tiles, sems, tile_sems) = refs[:many], refs[many:]
-        tile_copies = []
-        for part in range(moments // step):
-            for t in range(n):
-                source = a.at[pl.ds(part * step, step), :, :, pl.ds(t * width, width)]
-                copy = pltpu.make_async_copy(source, tiles.at[t, pl.ds(part * step, step)], tile_sems.at[part, t])
-                copy.start()
-                tile_copies.append(copy)
-        pairs = [(tile_of(a, me_ref, 1, width, 0, moments, slice(0, rows)), near.at[pl.ds(0, moments)])]
-        for r, far in enumerate(fars, 2):
-            pairs.append((tile_of(a, me_ref, r, width, FIRST, rest, slice(0, HALF)), far.at[pl.ds(0, rest)]))
-        copies = [pltpu.make_async_copy(source, o, sems.at[i]) for i, (source, o) in enumerate(pairs)]
+    parts = moments // step
+    low, high = slice(0, HALF), slice(HALF, 2 * HALF)
+
+    def kernel(me_ref, a, halo, near, *refs):
+        fars, (own, upper, found, sems) = refs[:many], refs[many:]
+        pieces = [(0, slice(0, rows), own), (1, slice(0, rows), near)]
+        for r in range(2, n):
+            pieces += [(r, low, fars[r - 2]), (r, high, upper.at[r - 2])]
+        copies = []
+        for part in range(parts):
+            for i, (r, row, ref) in enumerate(pieces):
+                source = tile_of(a, me_ref, r, width, part * step, step, row)
+                copies.append(pltpu.make_async_copy(source, ref.at[pl.ds(part * step, step)], sems.at[part, i]))
         for copy in copies:
             copy.start()
-        lane = lax.broadcasted_iota(jnp.int32, (share, rows, width), 2)
-        for copy in tile_copies:
-            copy.wait()
-        for r in range(n):
-            east = lax.rem((me_ref[0] ^ r) + 1, n)
-            total = jnp.zeros((share, rows, width), jnp.float32)
-            for m in range(moments):
-                kept = jnp.where(lane < MAXSUB, tiles[east, m], 0.0)
-                total = total + pltpu.roll(kept, MAXSUB * m, 2)
-            if r == 0:
-                halo[0] = total
-            elif r == 1:
-                near[moments] = total
-            else:
-                for g in range(extra):
-                    fars[r - 2][rest + g] = total[:, g * HALF : (g + 1) * HALF, :]
-        for copy in copies:
-            copy.wait()
+
+        totals = [jnp.zeros((share, row.stop - row.start, width), jnp.float32) for _, row, _ in pieces]
+        for part in range(parts):
+            for copy in copies[part * len(pieces) : (part + 1) * len(pieces)]:
+                copy.wait()
+            for i, (_, row, ref) in enumerate(pieces):
+                lane = lax.broadcasted_iota(jnp.int32, totals[i].shape, 2)
+                for m in range(part * step, (part + 1) * step):
+                    kept = jnp.where(lane < MAXSUB, ref[m], 0.0)
+                    totals[i] = totals[i] + (pltpu.roll(kept, MAXSUB * m, 2) if m else kept)
+        for (r, row, _), total in zip(pieces, totals):
+            west = lax.rem((me_ref[0] ^ r) + (n - 1), n) ^ me_ref[0]
+            found[west, :, row, :] = total
+        halo[0] = found[0]
+        near[moments] = found[1]
+        for r in range(2, n):
+            for g in range(rows // HALF):
+                fars[r - 2][moments + g] = found[r, :, g * HALF : (g + 1) * HALF, :]
 
     shapes = [f32(1, share, rows, width), f32(moments + 1, share, rows, width)]
-    shapes += [f32(rest + extra, share, HALF, width)] * many
+    shapes += [f32(moments + rows // HALF, share, HALF, width)] * many
     return call(
-        kernel, [SCALAR, FAR] + [ANY] * len(tokens), [me, adj, *tokens], [NEAR] * len(shapes), shapes, 1024, 1024, None,
+        kernel, [SCALAR, FAR], [me, adj], [NEAR] * len(shapes), shapes, 1024, 1024, None,
         [
-            pltpu.VMEM((n, moments, share, rows, width), jnp.float32),
-            pltpu.SemaphoreType.DMA((len(shapes),)),
-            pltpu.SemaphoreType.DMA((moments // step, n)),
+            pltpu.VMEM((moments, share, rows, width), jnp.float32),
+            pltpu.VMEM((many, moments, share, HALF, width), jnp.float32),
+            pltpu.VMEM((n, share, rows, width), jnp.float32),
+            pltpu.SemaphoreType.DMA((parts, 2 + 2 * many)),
         ],
         VMEM_WIDE,
     )
 
 
-def stencil(me, courant, halo, active, n, *tokens):
+def stencil(me, courant, halo, active, n):
     levels, rows, width = courant.shape
     share = levels // n
     per = width // MAXSUB
 
-    def kernel(me_ref, c_ref, h_ref, act_ref, *refs):
-        w_ref, p_ref = refs[len(tokens) :]
+    def kernel(me_ref, c_ref, h_ref, act_ref, w_ref, p_ref):
         lane = lax.broadcasted_iota(jnp.int32, (rows, width), 1)
         act = act_ref[...]
 
@@ -207,12 +200,12 @@
 
     size = levels * rows * width
     return call(
-        kernel, [SCALAR, NEAR, NEAR, NEAR] + [ANY] * len(tokens), [me, courant, halo, active, *tokens], [NEAR, NEAR],
-        [f32(MAXSUB + 1, levels, rows, width), f32(MAXSUB, levels, rows, width)], size * 300, size * 80, cost=STENCIL_COST,
-    )
-
-
-def beyond(halos, packed, first):
+        kernel, [SCALAR, NEAR, NEAR, NEAR], [me, courant, halo, active], [NEAR, NEAR],
+        [f32(MAXSUB + 1, levels, rows, width), f32(MAXSUB, levels, rows, width)], size * 300, size * 80,
+    )
+
+
+def beyond(halos, packed, first, token):
     share, width = halos[0].shape[1], halos[0].shape[3]
     levels, rows = packed.shape[1:3]
     count = len(halos)
@@ -237,17 +230,17 @@
 
     size = count * share * rows * width
     return call(
-        kernel, [block_of(h) for h in halos] + [pl.BlockSpec(packed.shape, lambda i: (0, 0, 0, 0))],
-        list(halos) + [packed], pl.BlockSpec((count * share, rows, width), lambda i: (0, 0, 0)),
+        kernel, [block_of(h) for h in halos] + [pl.BlockSpec(packed.shape, lambda i: (0, 0, 0, 0)), ANY],
+        list(halos) + [packed, token], pl.BlockSpec((count * share, rows, width), lambda i: (0, 0, 0)),
         f32(count * share, rows, width), size * 24, size * 40, grid=(1,),
     )
 
 
-def coefficients(me, courant_lat, mass, entrain, cloud, north, n):
+def coefficients(me, courant_lat, mass, entrain, cloud, north, n, token):
     levels, rows, width = mass.shape
     share = levels // n
 
-    def kernel(me_ref, lat_ref, mass_ref, entrain_ref, cloud_ref, north_ref, rate_ref, inside_ref, detrain_ref):
+    def kernel(me_ref, lat_ref, mass_ref, entrain_ref, cloud_ref, north_ref, _, rate_ref, inside_ref, detrain_ref):
         total = jnp.zeros((rows, width), jnp.float32)
         base, top = cloud_ref[0], cloud_ref[1]
         for r in range(n):
@@ -265,7 +258,7 @@
 
     size = levels * rows * width
     return call(
-        kernel, [SCALAR] + [NEAR] * 5, [me, courant_lat, mass, entrain, cloud, north], [NEAR] * 3,
+        kernel, [SCALAR] + [NEAR] * 5 + [ANY], [me, courant_lat, mass, entrain, cloud, north, token], [NEAR] * 3,
         [f32(levels, rows, width)] * 3, size * 10, size * 20,
     )
 
@@ -416,43 +409,37 @@
         return [swapped(b, r) for b, r in zip(blocks, partners)]
 
     south, upper = slice(0, HALF), slice(HALF, 2 * HALF)
-    rates = packed_rates(me, courant_lon)
-    firsts = taken(me, adj_in, width, [(r, 0, FIRST, south) for r in partners], rates)
-    rates = sent_west(rates)
-    firsts = exchanged([held_for(b, rates) for b in firsts])
-    own_halo, near, *rests = prepared(me, adj_in, width, n, firsts[0])
+    own_halo, near, *souths = prepared(me, adj_in, width, n)
+    rates = sent_west(packed_rates(courant_lon, own_halo))
+    souths = exchanged([held_for(b, rates) for b in souths])
     near = swapped(near, 1)
-    rests = exchanged(rests)
 
     active = jnp.broadcast_to(substeps[:, None], (rows, width))
     latitude = lax.axis_index("lat") * rows + jnp.arange(rows, dtype=jnp.int32)
     has_north = (latitude < rows * lax.axis_size("lat") - 1).astype(jnp.float32)
     has_north = jnp.broadcast_to(has_north[:, None], (rows, width))
-    rate, inside, detrain = coefficients(me, courant_lat, mass, entrain, cloud, has_north, n)
-    weights, packed = stencil(me, courant_lon, rates, active, n, rate, firsts[-1])
+    weights, packed = stencil(me, courant_lon, rates, active, n)
+    rate, inside, detrain = coefficients(me, courant_lat, mass, entrain, cloud, has_north, n, own_halo)
 
     whole = lambda i, me: (i, 0, 0, 0)
-    extra = beyond([own_halo, near], packed, 0)
+    extra = beyond([own_halo, near], packed, 0, rate)
     blocks = [(adj_in, lambda i, me: (i, 0, 0, me[0])), (near, whole)]
     close, edge_close = swept(me, blocks, 0, weights, extra, 0, moments, rows, 4)
     edge_close = sent_south(edge_close)
-    extra = beyond(rests, packed, 2)
-    lows = []
-    for start, size, arrays in ((0, FIRST, firsts), (FIRST, moments - FIRST, rests)):
-        low, edge = swept(me, [(array, whole) for array in arrays], 2, weights, extra, start, size, HALF, 4)
-        lows.append((low, start, sent_south(edge)))
+    extra = beyond(souths, packed, 2, rate)
+    low, edge = swept(me, [(array, whole) for array in souths], 2, weights, extra, 0, moments, HALF, 4)
+    edges = [edge_close, sent_south(edge)]
 
     parts, start = [], 0
     for size in NORTH_CHUNKS:
         parts += [(r, start, size, upper) for r in partners]
         start += size
-    sent = taken(me, adj_in, width, parts, firsts[-1])
+    sent = taken(me, adj_in, width, parts, souths[0], edge_close)
     out, start = None, 0
     for i, size in enumerate(NORTH_CHUNKS):
         blocks = exchanged(sent[i * (n - 2) : (i + 1) * (n - 2)])
-        low, offset, edge = lows[0] if start < FIRST else lows[1]
         out = finish(
-            me, out, start, size, close, low, offset, blocks, weights, extra, [edge_close, edge],
+            me, out, start, size, close, low, 0, blocks, weights, extra, edges,
             rate, inside, detrain, entrain, 2,
         )
         start += size

time: 67.6 us -> 61 us (0.902)
  starting transfers between devices: 16.9 us -> 14 us
  local copies, waits for them, and re-layouts: 4.01 us -> 1.28 us
  Pallas kernels: 29.4 us -> 28.4 us
    ppermute x11 -> x9, waiting for transfers between devices: 13.2 us -> 3.98 us  [swapped(): return lax.ppermute(block, 'lon', [(i, i ^ r) for i in range(n)])]
    ppermute x3 -> x2, waiting for transfers between devices: 1.18 us -> 9 us  [sent_south(): return lax.ppermute(block, 'lat', [(i + 1, i) for i in range(n - 1)])]
    unnamed x26 -> x16, local copies, waits for them, and re-layouts: 3.86 us -> 1.14 us
    pallas_call x10 -> x9, Pallas kernels: 14.1 us -> 12.2 us  [call(): pl.pallas_call(kernel, in_specs=in_specs, out_specs=out_specs, out_shape=...]
    ppermute x1, waiting for transfers between devices: 1.46 us -> 3.14 us  [sent_west(): return lax.ppermute(block, 'lon', [(i, (i - 1) % n) for i in range(n)])]
    ppermute x3 -> x2, starting transfers between devices: 5.98 us -> 4.3 us  [sent_south(): return lax.ppermute(block, 'lat', [(i + 1, i) for i in range(n - 1)])]
    pallas_call x6 -> x5, Pallas kernels: 15.3 us -> 16.2 us  [prefetched(): pl.pallas_call(kernel, grid_spec=pltpu.PrefetchScalarGridSpec(num_scalar_...]
    ppermute x11 -> x9, starting transfers between devices: 10.2 us -> 9.67 us  [swapped(): return lax.ppermute(block, 'lon', [(i, i ^ r) for i in range(n)])]
  transfers between devices with their start and end apart: 15 -> 12, of which waited for: 4 -> 6; matrix products, arithmetic and copies ran while one was open for 0% -> 0% of each run, Pallas kernels for 35% -> 38%
where the time goes in v3:
time: 61 us; the launch traced here: 60 us
  Pallas kernels  28.4 us (47%)
  waiting for transfers between devices  16.1 us (26%)
  starting transfers between devices  14 us (23%)
  local copies, waits for them, and re-layouts  1.28 us (2%)
    pallas_call x5, Pallas kernels, prefetched(): pl.pallas_call(kernel, grid_spec=pltpu.PrefetchScalarGridSpec(num_scalar_...  16.2 us
    pallas_call x9, Pallas kernels, call(): pl.pallas_call(kernel, in_specs=in_specs, out_specs=out_specs, out_shape=...  12.2 us
    ppermute x9, starting transfers between devices, swapped(): return lax.ppermute(block, 'lon', [(i, i ^ r) for i in range(n)])  9.67 us
    ppermute x2, waiting for transfers between devices, sent_south(): return lax.ppermute(block, 'lat', [(i + 1, i) for i in range(n - 1)])  9 us
    ppermute x2, starting transfers between devices, sent_south(): return lax.ppermute(block, 'lat', [(i + 1, i) for i in range(n - 1)])  4.3 us
    ppermute x9, waiting for transfers between devices, swapped(): return lax.ppermute(block, 'lon', [(i, i ^ r) for i in range(n)])  3.98 us
    ppermute x1, waiting for transfers between devices, sent_west(): return lax.ppermute(block, 'lon', [(i, (i - 1) % n) for i in range(n)])  3.14 us
  transfers between devices with their start and end apart: 12, of which 6 were waited for; matrix products, arithmetic and copies ran while one was open for 0% of the time, Pallas kernels for 38%

profile of v3, /device:TPU:5, one launch (start us, length us, event | category | flops | bytes accessed | tf_op | source)
XLA Modules:
  0.0 60.0 jit_solution(10974744206872804339)
XLA Ops:
  0.0 4.2 %shard_map.73 = (f32[1,8,16,128]{3,2,1,0:T(8,128)S(1)}, f32[17,8,16,128]{3,2,1,0:T(8,128)}, f32[18,8,8,128]{3,2,1,0:T(8,128)}, f32[18,8,8,128]{3,2,1,0:T(8,128)}) custom-call(s32[1]{0:T(128)} %bitcast.me_ref, f32[16,8,16,512]{3,2,1,0:T(8,128)} %a.3), custom_call_target="tpu_custom_call" | custom-call | flops 1024 | bytes 1024 | tf_op jit(solution)/shard_map/pallas_call | solution.py:44
  4.3 0.7 %collective-permute-start = (f32[17,8,16,128]{3,2,1,0:T(8,128)}, f32[17,8,16,128]{3,2,1,0:T(8,128)S(1)}, u32[]{:S(2)}, u32[]{:S(2)}) collective-permute-start(f32[17,8,16,128]{3,2,1,0:T(8,128)} %get-tuple-element.24), channel_id=1, source_target_pairs={{0,1},{1,0},{2,3},{3,2},{4,5},{5,4},{6,7},{7,6},{8,9},{9,8},{10,11... | collective-permute-start | bytes 3342344 | tf_op jit(solution)/shard_map/ppermute | solution.py:20
  5.2 3.1 %collective-permute-done.1.h_ref.t = f32[2,16,128]{2,1,0:T(8,128)S(1)} collective-permute-done((f32[2,16,128]{2,1,0:T(8,128)S(1)}, f32[2,16,128]{2,1,0:T(8,128)S(1)}, u32[]{:S(2)}, u32[]{:S(2)}) %collective-permute-start.1) | collective-permute-done | bytes 16416 | tf_op jit(solution)/shard_map/ppermute | solution.py:25
  8.4 1.2 %collective-permute-start.2 = (f32[18,8,8,128]{3,2,1,0:T(8,128)}, f32[18,8,8,128]{3,2,1,0:T(8,128)S(1)}, u32[]{:S(2)}, u32[]{:S(2)}) collective-permute-start(f32[18,8,8,128]{3,2,1,0:T(8,128)} %shard_map.79), channel_id=1, source_target_pairs={{0,2},{1,3},{2,0},{3,1},{4,6},{5,7},{6,4},{7,5},{8,10},{9,11},{10,... | collective-permute-start | bytes 1769480 | tf_op jit(solution)/shard_map/ppermute | solution.py:20
  10.2 1.1 %copy-done.2 = f32[32,16,128]{2,1,0:T(8,128)S(1)} copy-done((f32[32,16,128]{2,1,0:T(8,128)S(1)}, f32[32,16,128]{2,1,0:T(8,128)}, u32[]{:S(2)}) %copy-start.2) | copy-done | bytes 262168
  11.3 5.1 %shard_map.75 = (f32[9,32,16,128]{3,2,1,0:T(8,128)S(1)}, f32[8,32,16,128]{3,2,1,0:T(8,128)S(1)}) custom-call(s32[1]{0:T(128)} %bitcast.me_ref, f32[32,16,128]{2,1,0:T(8,128)S(1)} %copy-done.2, f32[2,16,128]{2,1,0:T(8,128)S(1)} %collective-permute-done.1.h_ref.t, s32[16,128]{1,0:T(8,128)S(1)} %broadcast_in_dim.7.act_ref), custom_call_target="tpu_custom_call" | custom-call | flops 1024 | bytes 1024 | tf_op jit(solution)/shard_map/pallas_call | solution.py:44
  16.7 5.4 %shard_map.78 = (f32[16,16,16,128]{3,2,1,0:T(8,128)S(1)}, f32[16,16,128]{2,1,0:T(8,128)S(1)}) custom-call(s32[1]{0:T(128)} %bitcast.me_ref, f32[16,8,16,512]{3,2,1,0:T(8,128)S(1)} %copy-done, f32[17,8,16,128]{3,2,1,0:T(8,128)S(1)} %collective-permute-done.refs_1_, f32[9,32,16,128]{3,2,1,0:T(8,128)S(1)} %get-tuple-element.26.refs_2_, ...), custom_call_target="tpu_custom_call" | custom-call | flops 1024 | bytes 1024 | tf_op jit(solution)/shard_map/pallas_call | solution.py:317
  22.1 2.1 %collective-permute-start.4 = (f32[16,16,128]{2,1,0:T(8,128)S(1)}, f32[16,16,128]{2,1,0:T(8,128)S(1)}, u32[]{:S(2)}, u32[]{:S(2)}) collective-permute-start(f32[16,16,128]{2,1,0:T(8,128)S(1)} %get-tuple-element.33), channel_id=1, source_target_pairs={{4,0},{8,4},{12,8},{16,12},{20,16},{24,20},{28,24},{5,1},{9,5},{13... | collective-permute-start | bytes 393224 | tf_op jit(solution)/shard_map/ppermute | solution.py:30
  24.2 5.4 %collective-permute-done.4.refs_1_.refs_4_ = f32[16,16,128]{2,1,0:T(8,128)S(1)} collective-permute-done((f32[16,16,128]{2,1,0:T(8,128)S(1)}, f32[16,16,128]{2,1,0:T(8,128)S(1)}, u32[]{:S(2)}, u32[]{:S(2)}) %collective-permute-start.4) | collective-permute-done | bytes 131104 | tf_op jit(solution)/shard_map/ppermute | solution.py:30
  29.6 1.2 %shard_map.83 = (f32[10,8,8,128]{3,2,1,0:T(8,128)S(1)}, f32[10,8,8,128]{3,2,1,0:T(8,128)S(1)}, f32[4,8,8,128]{3,2,1,0:T(8,128)S(1)}, f32[4,8,8,128]{3,2,1,0:T(8,...) custom-call(s32[1]{0:T(128)} %bitcast.me_ref, f32[16,8,16,512]{3,2,1,0:T(8,128)} %a.3, ...), custom_call_target="tpu_custom_call" | custom-call | flops 1024 | bytes 1024 | tf_op jit(solution)/shard_map/pallas_call | solution.py:44
  31.1 2.6 %collective-permute-start.11 = (f32[10,8,8,128]{3,2,1,0:T(8,128)S(1)}, f32[10,8,8,128]{3,2,1,0:T(8,128)S(1)}, u32[]{:S(2)}, u32[]{:S(2)}) collective-permute-start(f32[10,8,8,128]{3,2,1,0:T(8,128)S(1)} %get-tuple-element.42), channel_id=1, source_target_pairs={{0,3},{1,2},{2,1},{3,0},{4,7},{5,6},{6,5},{7,4},{8,11},{9,10},{10,... | collective-permute-start | bytes 983048 | tf_op jit(solution)/shard_map/ppermute | solution.py:20
  33.7 2.9 %collective-permute-done.3.refs_1_ = f32[18,8,8,128]{3,2,1,0:T(8,128)} collective-permute-done((f32[18,8,8,128]{3,2,1,0:T(8,128)}, f32[18,8,8,128]{3,2,1,0:T(8,128)}, u32[]{:S(2)}, u32[]{:S(2)}) %collective-permute-start.3) | collective-permute-done | bytes 589856 | tf_op jit(solution)/shard_map/ppermute | solution.py:20
  36.6 1.1 %shard_map.81.refs_3_ = f32[16,16,128]{2,1,0:T(8,128)S(1)} custom-call(f32[18,8,8,128]{3,2,1,0:T(8,128)S(1)} %collective-permute-done.2.refs_0_, f32[18,8,8,128]{3,2,1,0:T(8,128)} %collective-permute-done.3.refs_1_, f32[8,32,16,128]{3,2,1,0:T(8,128)S(1)} %get-tuple-element.27.refs_2_, f32[32,16,128]{2,1,0:T(8,128)S(1)} %get-tuple-element.28.refs_3_.refs_6_), custom_call_target="tpu_custom_call" | custom-call | flops 1024 | bytes 1024 | tf_op jit(solution)/shard_map/pallas_call | solution.py:44
  37.8 4.0 %shard_map.82 = (f32[16,16,8,128]{3,2,1,0:T(8,128)S(1)}, f32[16,16,128]{2,1,0:T(8,128)S(1)}) custom-call(s32[1]{0:T(128)} %bitcast.me_ref, f32[18,8,8,128]{3,2,1,0:T(8,128)S(1)} %collective-permute-done.2.refs_0_, f32[18,8,8,128]{3,2,1,0:T(8,128)} %collective-permute-done.3.refs_1_, f32[9,32,16,128]{3,2,1,0:T(8,128)S(1)} %get-tuple-element.26.refs_2_, ...), custom_call_target="tpu_custom_call" | custom-call | flops 1024 | bytes 1024 | tf_op jit(solution)/shard_map/pallas_call | solution.py:317
  41.8 2.2 %collective-permute-start.7 = (f32[16,16,128]{2,1,0:T(8,128)S(1)}, f32[16,16,128]{2,1,0:T(8,128)S(1)}, u32[]{:S(2)}, u32[]{:S(2)}) collective-permute-start(f32[16,16,128]{2,1,0:T(8,128)S(1)} %get-tuple-element.36), channel_id=1, source_target_pairs={{4,0},{8,4},{12,8},{16,12},{20,16},{24,20},{28,24},{5,1},{9,5},{13... | collective-permute-start | bytes 393224 | tf_op jit(solution)/shard_map/ppermute | solution.py:30
  43.9 1.1 %collective-permute-start.8 = (f32[4,8,8,128]{3,2,1,0:T(8,128)S(1)}, f32[4,8,8,128]{3,2,1,0:T(8,128)S(1)}, u32[]{:S(2)}, u32[]{:S(2)}) collective-permute-start(f32[4,8,8,128]{3,2,1,0:T(8,128)S(1)} %get-tuple-element.39), channel_id=1, source_target_pairs={{0,2},{1,3},{2,0},{3,1},{4,6},{5,7},{6,4},{7,5},{8,10},{9,11},{10,... | collective-permute-start | bytes 393224 | tf_op jit(solution)/shard_map/ppermute | solution.py:20
  45.0 0.9 %collective-permute-start.9 = (f32[4,8,8,128]{3,2,1,0:T(8,128)S(1)}, f32[4,8,8,128]{3,2,1,0:T(8,128)S(1)}, u32[]{:S(2)}, u32[]{:S(2)}) collective-permute-start(f32[4,8,8,128]{3,2,1,0:T(8,128)S(1)} %get-tuple-element.40), channel_id=1, source_target_pairs={{0,3},{1,2},{2,1},{3,0},{4,7},{5,6},{6,5},{7,4},{8,11},{9,10},{10,... | collective-permute-start | bytes 393224 | tf_op jit(solution)/shard_map/ppermute | solution.py:20
  45.9 3.6 %collective-permute-done.7.refs_5_ = f32[16,16,128]{2,1,0:T(8,128)S(1)} collective-permute-done((f32[16,16,128]{2,1,0:T(8,128)S(1)}, f32[16,16,128]{2,1,0:T(8,128)S(1)}, u32[]{:S(2)}, u32[]{:S(2)}) %collective-permute-start.7) | collective-permute-done | bytes 131104 | tf_op jit(solution)/shard_map/ppermute | solution.py:30
  49.5 0.5 collective-permute-start.5
  50.0 2.1 %collective-permute-start.6 = (f32[2,8,8,128]{3,2,1,0:T(8,128)S(1)}, f32[2,8,8,128]{3,2,1,0:T(8,128)S(1)}, u32[]{:S(2)}, u32[]{:S(2)}) collective-permute-start(f32[2,8,8,128]{3,2,1,0:T(8,128)S(1)} %get-tuple-element.35), channel_id=1, source_target_pairs={{0,3},{1,2},{2,1},{3,0},{4,7},{5,6},{6,5},{7,4},{8,11},{9,10},{10,... | collective-permute-start | bytes 196616 | tf_op jit(solution)/shard_map/ppermute | solution.py:20
  52.1 3.9 %shard_map.84.refs_10_ = f32[16,32,16,128]{3,2,1,0:T(8,128)} custom-call(s32[1]{0:T(128)} %bitcast.me_ref, f32[16,16,16,128]{3,2,1,0:T(8,128)S(1)} %get-tuple-element.29.close_ref, f32[16,16,8,128]{3,2,1,0:T(8,128)S(1)} %get-tuple-element.32.low_ref, f32[10,8,8,128]{3,2,1,0:T(8,128)S(1)} %collective-permute-done.10.refs_0_, ...), custom_call_target="tpu_custom_call" | custom-call | flops 1024 | bytes 1024 | tf_op jit(solution)/shard_map/pallas_call | solution.py:317
  56.2 1.8 %shard_map.85.refs_10_ = f32[16,32,16,128]{3,2,1,0:T(8,128)} custom-call(s32[1]{0:T(128)} %bitcast.me_ref, f32[16,16,16,128]{3,2,1,0:T(8,128)S(1)} %get-tuple-element.29.close_ref, f32[16,16,8,128]{3,2,1,0:T(8,128)S(1)} %get-tuple-element.32.low_ref, f32[4,8,8,128]{3,2,1,0:T(8,128)S(1)} %collective-permute-done.8.refs_0_, ...), custom_call_target="tpu_custom_call", output_to_operand_aliasing={{}: (13, {})} | custom-call | flops 1024 | bytes 1024 | tf_op jit(solution)/shard_map/pallas_call | solution.py:317
  58.0 0.8 %collective-permute-done.6.refs_1_ = f32[2,8,8,128]{3,2,1,0:T(8,128)S(1)} collective-permute-done((f32[2,8,8,128]{3,2,1,0:T(8,128)S(1)}, f32[2,8,8,128]{3,2,1,0:T(8,128)S(1)}, u32[]{:S(2)}, u32[]{:S(2)}) %collective-permute-start.6) | collective-permute-done | bytes 65568 | tf_op jit(solution)/shard_map/ppermute | solution.py:20
  58.8 1.3 %shard_map.86 = f32[16,32,16,128]{3,2,1,0:T(8,128)} custom-call(s32[1]{0:T(128)} %bitcast.me_ref, f32[16,16,16,128]{3,2,1,0:T(8,128)S(1)} %get-tuple-element.29.close_ref, f32[16,16,8,128]{3,2,1,0:T(8,128)S(1)} %get-tuple-element.32.low_ref, f32[2,8,8,128]{3,2,1,0:T(8,128)S(1)} %collective-permute-done.5.refs_0_, ...), custom_call_target="tpu_custom_call", output_to_operand_aliasing={{}: (13, {})} | custom-call | flops 1024 | bytes 1024 | tf_op jit(solution)/shard_map/pallas_call | solution.py:317
  (33 shorter events, 1.7 us)
Async XLA Ops:
  0.0 5.0 %copy-start.1 = (f32[32,16,128]{2,1,0:T(8,128)S(1)}, f32[32,16,128]{2,1,0:T(8,128)}, u32[]{:S(2)}) copy-start(f32[32,16,128]{2,1,0:T(8,128)} %c_ref.1) | copy-start | bytes 786436
  4.2 5.8 %copy-start.3 = (f32[32,16,128]{2,1,0:T(8,128)S(1)}, f32[32,16,128]{2,1,0:T(8,128)}, u32[]{:S(2)}) copy-start(f32[32,16,128]{2,1,0:T(8,128)} %lat_ref.1) | copy-start | bytes 786436
  4.2 5.7 %copy-start.4 = (f32[32,16,128]{2,1,0:T(8,128)S(1)}, f32[32,16,128]{2,1,0:T(8,128)}, u32[]{:S(2)}) copy-start(f32[32,16,128]{2,1,0:T(8,128)} %mass_ref.1) | copy-start | bytes 786436
  4.2 5.7 %copy-start.5 = (f32[16,128]{1,0:T(8,128)S(1)}, f32[16,128]{1,0:T(8,128)}, u32[]{:S(2)}) copy-start(f32[16,128]{1,0:T(8,128)} %refs_9_.5) | copy-start | bytes 24580
  4.3 5.7 %copy-start.6 = (s32[2,16,128]{2,1,0:T(8,128)S(1)}, s32[2,16,128]{2,1,0:T(8,128)}, u32[]{:S(2)}) copy-start(s32[2,16,128]{2,1,0:T(8,128)} %cloud_ref.1) | copy-start | bytes 49156
  4.3 5.8 %copy-start.7 = (s32[16]{0:T(128)S(1)}, s32[16]{0:T(128)}, u32[]{:S(2)}) copy-start(s32[16]{0:T(128)} %param.13) | copy-start | bytes 196
  4.3 12.1 %collective-permute-start = (f32[17,8,16,128]{3,2,1,0:T(8,128)}, f32[17,8,16,128]{3,2,1,0:T(8,128)S(1)}, u32[]{:S(2)}, u32[]{:S(2)}) collective-permute-start(f32[17,8,16,128]{3,2,1,0:T(8,128)} %get-tuple-element.24), channel_id=1, source_target_pairs={{0,1},{1,0},{2,3},{3,2},{4,5},{5,4},{6,7},{7,6},{8,9},{9,8},{10,11... | collective-permute-start | bytes 3342344 | tf_op jit(solution)/shard_map/ppermute | solution.py:20
  5.2 3.2 %collective-permute-start.1 = (f32[2,16,128]{2,1,0:T(8,128)S(1)}, f32[2,16,128]{2,1,0:T(8,128)S(1)}, u32[]{:S(2)}, u32[]{:S(2)}) collective-permute-start(f32[2,16,128]{2,1,0:T(8,128)S(1)} %shard_map.74), channel_id=1, source_target_pairs={{0,3},{1,0},{2,1},{3,2},{4,7},{5,4},{6,5},{7,6},{8,11},{9,8},{10,9... | collective-permute-start | bytes 49160 | tf_op jit(solution)/shard_map/ppermute | solution.py:25
  8.4 15.8 %collective-permute-start.2 = (f32[18,8,8,128]{3,2,1,0:T(8,128)}, f32[18,8,8,128]{3,2,1,0:T(8,128)S(1)}, u32[]{:S(2)}, u32[]{:S(2)}) collective-permute-start(f32[18,8,8,128]{3,2,1,0:T(8,128)} %shard_map.79), channel_id=1, source_target_pairs={{0,2},{1,3},{2,0},{3,1},{4,6},{5,7},{6,4},{7,5},{8,10},{9,11},{10,... | collective-permute-start | bytes 1769480 | tf_op jit(solution)/shard_map/ppermute | solution.py:20
  9.6 27.0 %collective-permute-start.3 = (f32[18,8,8,128]{3,2,1,0:T(8,128)}, f32[18,8,8,128]{3,2,1,0:T(8,128)}, u32[]{:S(2)}, u32[]{:S(2)}) collective-permute-start(f32[18,8,8,128]{3,2,1,0:T(8,128)} %shard_map.80), channel_id=1, source_target_pairs={{0,3},{1,2},{2,1},{3,0},{4,7},{5,6},{6,5},{7,4},{8,11},{9,10},{10,... | collective-permute-start | bytes 1769480 | tf_op jit(solution)/shard_map/ppermute | solution.py:20
  9.9 6.8 %copy-start = (f32[16,8,16,512]{3,2,1,0:T(8,128)S(1)}, f32[16,8,16,512]{3,2,1,0:T(8,128)}, u32[]{:S(2)}) copy-start(f32[16,8,16,512]{3,2,1,0:T(8,128)} %a.3) | copy-start | bytes 12582916
  10.2 1.1 %copy-start.2 = (f32[32,16,128]{2,1,0:T(8,128)S(1)}, f32[32,16,128]{2,1,0:T(8,128)}, u32[]{:S(2)}) copy-start(f32[32,16,128]{2,1,0:T(8,128)} %c_ref.1) | copy-start | bytes 786436
  22.1 7.5 %collective-permute-start.4 = (f32[16,16,128]{2,1,0:T(8,128)S(1)}, f32[16,16,128]{2,1,0:T(8,128)S(1)}, u32[]{:S(2)}, u32[]{:S(2)}) collective-permute-start(f32[16,16,128]{2,1,0:T(8,128)S(1)} %get-tuple-element.33), channel_id=1, source_target_pairs={{4,0},{8,4},{12,8},{16,12},{20,16},{24,20},{28,24},{5,1},{9,5},{13... | collective-permute-start | bytes 393224 | tf_op jit(solution)/shard_map/ppermute | solution.py:30
  30.8 19.2 %collective-permute-start.10 = (f32[10,8,8,128]{3,2,1,0:T(8,128)S(1)}, f32[10,8,8,128]{3,2,1,0:T(8,128)S(1)}, u32[]{:S(2)}, u32[]{:S(2)}) collective-permute-start(f32[10,8,8,128]{3,2,1,0:T(8,128)S(1)} %get-tuple-element.41), channel_id=1, source_target_pairs={{0,2},{1,3},{2,0},{3,1},{4,6},{5,7},{6,4},{7,5},{8,10},{9,11},{10,... | collective-permute-start | bytes 983048 | tf_op jit(solution)/shard_map/ppermute | solution.py:20
  31.1 21.0 %collective-permute-start.11 = (f32[10,8,8,128]{3,2,1,0:T(8,128)S(1)}, f32[10,8,8,128]{3,2,1,0:T(8,128)S(1)}, u32[]{:S(2)}, u32[]{:S(2)}) collective-permute-start(f32[10,8,8,128]{3,2,1,0:T(8,128)S(1)} %get-tuple-element.42), channel_id=1, source_target_pairs={{0,3},{1,2},{2,1},{3,0},{4,7},{5,6},{6,5},{7,4},{8,11},{9,10},{10,... | collective-permute-start | bytes 983048 | tf_op jit(solution)/shard_map/ppermute | solution.py:20
  41.8 7.7 %collective-permute-start.7 = (f32[16,16,128]{2,1,0:T(8,128)S(1)}, f32[16,16,128]{2,1,0:T(8,128)S(1)}, u32[]{:S(2)}, u32[]{:S(2)}) collective-permute-start(f32[16,16,128]{2,1,0:T(8,128)S(1)} %get-tuple-element.36), channel_id=1, source_target_pairs={{4,0},{8,4},{12,8},{16,12},{20,16},{24,20},{28,24},{5,1},{9,5},{13... | collective-permute-start | bytes 393224 | tf_op jit(solution)/shard_map/ppermute | solution.py:30
  43.9 12.0 %collective-permute-start.8 = (f32[4,8,8,128]{3,2,1,0:T(8,128)S(1)}, f32[4,8,8,128]{3,2,1,0:T(8,128)S(1)}, u32[]{:S(2)}, u32[]{:S(2)}) collective-permute-start(f32[4,8,8,128]{3,2,1,0:T(8,128)S(1)} %get-tuple-element.39), channel_id=1, source_target_pairs={{0,2},{1,3},{2,0},{3,1},{4,6},{5,7},{6,4},{7,5},{8,10},{9,11},{10,... | collective-permute-start | bytes 393224 | tf_op jit(solution)/shard_map/ppermute | solution.py:20
  45.0 11.2 %collective-permute-start.9 = (f32[4,8,8,128]{3,2,1,0:T(8,128)S(1)}, f32[4,8,8,128]{3,2,1,0:T(8,128)S(1)}, u32[]{:S(2)}, u32[]{:S(2)}) collective-permute-start(f32[4,8,8,128]{3,2,1,0:T(8,128)S(1)} %get-tuple-element.40), channel_id=1, source_target_pairs={{0,3},{1,2},{2,1},{3,0},{4,7},{5,6},{6,5},{7,4},{8,11},{9,10},{10,... | collective-permute-start | bytes 393224 | tf_op jit(solution)/shard_map/ppermute | solution.py:20
  49.5 8.5 %collective-permute-start.5 = (f32[2,8,8,128]{3,2,1,0:T(8,128)S(1)}, f32[2,8,8,128]{3,2,1,0:T(8,128)S(1)}, u32[]{:S(2)}, u32[]{:S(2)}) collective-permute-start(f32[2,8,8,128]{3,2,1,0:T(8,128)S(1)} %get-tuple-element.34), channel_id=1, source_target_pairs={{0,2},{1,3},{2,0},{3,1},{4,6},{5,7},{6,4},{7,5},{8,10},{9,11},{10,... | collective-permute-start | bytes 196616 | tf_op jit(solution)/shard_map/ppermute | solution.py:20
  50.0 8.8 %collective-permute-start.6 = (f32[2,8,8,128]{3,2,1,0:T(8,128)S(1)}, f32[2,8,8,128]{3,2,1,0:T(8,128)S(1)}, u32[]{:S(2)}, u32[]{:S(2)}) collective-permute-start(f32[2,8,8,128]{3,2,1,0:T(8,128)S(1)} %get-tuple-element.35), channel_id=1, source_target_pairs={{0,3},{1,2},{2,1},{3,0},{4,7},{5,6},{6,5},{7,4},{8,11},{9,10},{10,... | collective-permute-start | bytes 196616 | tf_op jit(solution)/shard_map/ppermute | solution.py:20

commit v4 on v3

--- a/solution.py
+++ b/solution.py
@@ -12,6 +12,7 @@
 VMEM_LIMIT = 12 * 1024 * 1024
 COST = 1024
 VMEM_WIDE = 50 * 1024 * 1024
+FIRST = 4
 NORTH_CHUNKS = (10, 4, 2)
 
 
@@ -59,11 +60,11 @@
     return adj.at[pl.ds(first, count), :, rows, pl.ds(start, width)]
 
 
-def held_for(block, token):
-    def kernel(b, t, o):
+def held_for(block, *tokens):
+    def kernel(*refs):
         pass
 
-    return call(kernel, [ANY, ANY], [block, token], ANY, f32(*block.shape), 0, 0, {0: 0})
+    return call(kernel, [ANY] * (1 + len(tokens)), [block, *tokens], ANY, f32(*block.shape), 0, 0, {0: 0})
 
 
 def taken(me, adj, width, parts, *tokens):
@@ -104,21 +105,28 @@
 
 def prepared(me, adj, width, n):
     moments, share, rows, _ = adj.shape
-    step = 4
+    step = FIRST
     many = n - 2
     parts = moments // step
+    rest = moments - FIRST
     low, high = slice(0, HALF), slice(HALF, 2 * HALF)
 
     def kernel(me_ref, a, halo, near, *refs):
-        fars, (own, upper, found, sems) = refs[:many], refs[many:]
+        fars, (own, upper, early, found, sems) = refs[:many], refs[many:]
+
+        def block_of(ref, r, part):
+            if ref is None:
+                return early.at[r - 2] if part == 0 else fars[r - 2].at[pl.ds((part - 1) * step, step)]
+            return ref.at[pl.ds(part * step, step)]
+
         pieces = [(0, slice(0, rows), own), (1, slice(0, rows), near)]
         for r in range(2, n):
-            pieces += [(r, low, fars[r - 2]), (r, high, upper.at[r - 2])]
+            pieces += [(r, low, None), (r, high, upper.at[r - 2])]
         copies = []
         for part in range(parts):
             for i, (r, row, ref) in enumerate(pieces):
                 source = tile_of(a, me_ref, r, width, part * step, step, row)
-                copies.append(pltpu.make_async_copy(source, ref.at[pl.ds(part * step, step)], sems.at[part, i]))
+                copies.append(pltpu.make_async_copy(source, block_of(ref, r, part), sems.at[part, i]))
         for copy in copies:
             copy.start()
 
@@ -126,10 +134,11 @@
         for part in range(parts):
             for copy in copies[part * len(pieces) : (part + 1) * len(pieces)]:
                 copy.wait()
-            for i, (_, row, ref) in enumerate(pieces):
+            for i, (r, row, ref) in enumerate(pieces):
                 lane = lax.broadcasted_iota(jnp.int32, totals[i].shape, 2)
+                block = block_of(ref, r, part)
                 for m in range(part * step, (part + 1) * step):
-                    kept = jnp.where(lane < MAXSUB, ref[m], 0.0)
+                    kept = jnp.where(lane < MAXSUB, block[m - part * step], 0.0)
                     totals[i] = totals[i] + (pltpu.roll(kept, MAXSUB * m, 2) if m else kept)
         for (r, row, _), total in zip(pieces, totals):
             west = lax.rem((me_ref[0] ^ r) + (n - 1), n) ^ me_ref[0]
@@ -138,15 +147,16 @@
         near[moments] = found[1]
         for r in range(2, n):
             for g in range(rows // HALF):
-                fars[r - 2][moments + g] = found[r, :, g * HALF : (g + 1) * HALF, :]
+                fars[r - 2][rest + g] = found[r, :, g * HALF : (g + 1) * HALF, :]
 
     shapes = [f32(1, share, rows, width), f32(moments + 1, share, rows, width)]
-    shapes += [f32(moments + rows // HALF, share, HALF, width)] * many
+    shapes += [f32(rest + rows // HALF, share, HALF, width)] * many
     return call(
         kernel, [SCALAR, FAR], [me, adj], [NEAR] * len(shapes), shapes, 1024, 1024, None,
         [
             pltpu.VMEM((moments, share, rows, width), jnp.float32),
             pltpu.VMEM((many, moments, share, HALF, width), jnp.float32),
+            pltpu.VMEM((many, FIRST, share, HALF, width), jnp.float32),
             pltpu.VMEM((n, share, rows, width), jnp.float32),
             pltpu.SemaphoreType.DMA((parts, 2 + 2 * many)),
         ],
@@ -275,14 +285,15 @@
     return jnp.stack([jnp.where(past, pltpu.roll(packed, shift - MAXSUB * m, 1), 0.0) for m in range(step)])
 
 
-def swept(me, blocks, first, weights, extra, start, moments, rows, step):
+def swept(me, blocks, first, weights, extra, start, moments, rows, step, heads=()):
     count = len(blocks)
     levels, width = weights.shape[1], weights.shape[3]
     size = extra.shape[0]
     share = size // count
 
     def kernel(me_ref, *refs):
-        a, (w_ref, x_ref, o, e) = refs[:count], refs[count:]
+        a, h, (w_ref, x_ref, o, e) = refs[:count], refs[count : count + len(heads)], refs[count + len(heads) :]
+        head = pl.program_id(0) == 0
         past = lax.broadcasted_iota(jnp.int32, (HALF, width), 1) >= width - MAXSUB
         shift = width - MAXSUB - MAXSUB * (start + pl.program_id(0) * step)
         for g in range(rows // HALF):
@@ -290,13 +301,17 @@
             for r in range(count):
                 for l in range(share):
                     k = r * share + l
-                    x = stepped(a[r][:, l, part, :], [w_ref[q, first * share + k, part, :] for q in range(MAXSUB + 1)])
+                    x = a[r][:, l, part, :]
+                    if heads:
+                        x = jnp.where(head, h[r][:, l, part, :], x)
+                    x = stepped(x, [w_ref[q, first * share + k, part, :] for q in range(MAXSUB + 1)])
                     x = x + added(x_ref[k, part, :], shift, past, step)
                     o[:, k, part, :] = x
                     if g == 0:
                         e[:, k : k + 1, :] = x[:, :1, :]
 
     in_specs = [pl.BlockSpec((step, share, rows, width), index) for _, index in blocks]
+    in_specs += [pl.BlockSpec((step, share, rows, width), lambda i, me: (0, 0, 0, 0))] * len(heads)
     in_specs += [
         pl.BlockSpec((MAXSUB + 1, levels, rows, width), lambda i, me: (0, 0, 0, 0)),
         pl.BlockSpec((size, rows, width), lambda i, me: (0, 0, 0)),
@@ -309,7 +324,7 @@
             pl.BlockSpec((step, size, width), lambda i, me: (i, 0, 0)),
         ],
         [f32(moments, size, rows, width), f32(moments, size, width)],
-        [me] + [array for array, _ in blocks] + [weights, extra], work * 25, work * 8,
+        [me] + [array for array, _ in blocks] + list(heads) + [weights, extra], work * 25, work * 8,
     )
 
 
@@ -409,10 +424,11 @@
         return [swapped(b, r) for b, r in zip(blocks, partners)]
 
     south, upper = slice(0, HALF), slice(HALF, 2 * HALF)
+    firsts = exchanged(taken(me, adj_in, width, [(r, 0, FIRST, south) for r in partners]))
+    rates = sent_west(packed_rates(courant_lon, me))
     own_halo, near, *souths = prepared(me, adj_in, width, n)
-    rates = sent_west(packed_rates(courant_lon, own_halo))
-    souths = exchanged([held_for(b, rates) for b in souths])
-    near = swapped(near, 1)
+    near = swapped(held_for(near, rates, *firsts), 1)
+    souths = exchanged([held_for(b, rates, *firsts) for b in souths])
 
     active = jnp.broadcast_to(substeps[:, None], (rows, width))
     latitude = lax.axis_index("lat") * rows + jnp.arange(rows, dtype=jnp.int32)
@@ -426,15 +442,16 @@
     blocks = [(adj_in, lambda i, me: (i, 0, 0, me[0])), (near, whole)]
     close, edge_close = swept(me, blocks, 0, weights, extra, 0, moments, rows, 4)
     edge_close = sent_south(edge_close)
-    extra = beyond(souths, packed, 2, rate)
-    low, edge = swept(me, [(array, whole) for array in souths], 2, weights, extra, 0, moments, HALF, 4)
+    extra = beyond(souths, packed, 2, edge_close)
+    later = lambda i, me: (jnp.maximum(i - 1, 0), 0, 0, 0)
+    low, edge = swept(me, [(array, later) for array in souths], 2, weights, extra, 0, moments, HALF, FIRST, firsts)
     edges = [edge_close, sent_south(edge)]
 
     parts, start = [], 0
     for size in NORTH_CHUNKS:
         parts += [(r, start, size, upper) for r in partners]
         start += size
-    sent = taken(me, adj_in, width, parts, souths[0], edge_close)
+    sent = taken(me, adj_in, width, parts, souths[0], close)
     out, start = None, 0
     for i, size in enumerate(NORTH_CHUNKS):
         blocks = exchanged(sent[i * (n - 2) : (i + 1) * (n - 2)])

time: 61 us -> 56.9 us (0.933); the launches traced: 60 us -> 56.6 us
  waiting for transfers between devices: 16.1 us -> 9.08 us
  starting transfers between devices: 14 us -> 16.6 us
  Pallas kernels: 28.4 us -> 29.3 us
    ppermute x2, waiting for transfers between devices: 9 us -> 3.6 us  [sent_south(): return lax.ppermute(block, 'lat', [(i + 1, i) for i in range(n - 1)])]
    ppermute x9 -> x11, starting transfers between devices: 9.67 us -> 12.5 us  [swapped(): return lax.ppermute(block, 'lon', [(i, i ^ r) for i in range(n)])]
    ppermute x1, waiting for transfers between devices: 3.14 us -> 1.63 us  [sent_west(): return lax.ppermute(block, 'lon', [(i, (i - 1) % n) for i in range(n)])]
    pallas_call x9 -> x11, Pallas kernels: 12.2 us -> 13.1 us  [call(): pl.pallas_call(kernel, in_specs=in_specs, out_specs=out_specs, out_shape=...]
    ppermute x9 -> x11, waiting for transfers between devices: 3.98 us -> 3.85 us  [swapped(): return lax.ppermute(block, 'lon', [(i, i ^ r) for i in range(n)])]
  transfers between devices with their start and end apart: 12 -> 14, of which waited for: 6 -> 4; matrix products, arithmetic and copies ran while one was open for 0% -> 0% of each run, Pallas kernels for 38% -> 48%
where the time goes in v4:
time: 56.9 us; the launch traced here: 56.6 us
  Pallas kernels  29.3 us (51%)
  starting transfers between devices  16.6 us (29%)
  waiting for transfers between devices  9.08 us (16%)
  local copies, waits for them, and re-layouts  1.29 us (2%)
    pallas_call x5, Pallas kernels, prefetched(): pl.pallas_call(kernel, grid_spec=pltpu.PrefetchScalarGridSpec(num_scalar_...  16.3 us
    pallas_call x11, Pallas kernels, call(): pl.pallas_call(kernel, in_specs=in_specs, out_specs=out_specs, out_shape=...  13.1 us
    ppermute x11, starting transfers between devices, swapped(): return lax.ppermute(block, 'lon', [(i, i ^ r) for i in range(n)])  12.5 us
    ppermute x2, starting transfers between devices, sent_south(): return lax.ppermute(block, 'lat', [(i + 1, i) for i in range(n - 1)])  4.06 us
    ppermute x11, waiting for transfers between devices, swapped(): return lax.ppermute(block, 'lon', [(i, i ^ r) for i in range(n)])  3.85 us
    ppermute x2, waiting for transfers between devices, sent_south(): return lax.ppermute(block, 'lat', [(i + 1, i) for i in range(n - 1)])  3.6 us
    ppermute x1, waiting for transfers between devices, sent_west(): return lax.ppermute(block, 'lon', [(i, (i - 1) % n) for i in range(n)])  1.63 us
    unnamed x20, local copies, waits for them, and re-layouts  1.15 us
  transfers between devices with their start and end apart: 14, of which 4 were waited for; matrix products, arithmetic and copies ran while one was open for 0% of the time, Pallas kernels for 48%

profile of v4, /device:TPU:5, one launch (start us, length us, event | category | flops | bytes accessed | tf_op | source)
XLA Modules:
  0.0 56.6 jit_solution(13989378917317820201)
XLA Ops:
  0.0 1.0 %shard_map.75 = (f32[4,8,8,128]{3,2,1,0:T(8,128)S(1)}, f32[4,8,8,128]{3,2,1,0:T(8,128)S(1)}) custom-call(s32[1]{0:T(128)} %bitcast.me_ref._, f32[16,8,16,512]{3,2,1,0:T(8,128)} %a.5), custom_call_target="tpu_custom_call" | custom-call | flops 1024 | bytes 1024 | tf_op jit(solution)/shard_map/pallas_call | solution.py:45
  1.0 1.3 %collective-permute-start.1 = (f32[4,8,8,128]{3,2,1,0:T(8,128)S(1)}, f32[4,8,8,128]{3,2,1,0:T(8,128)S(1)}, u32[]{:S(2)}, u32[]{:S(2)}) collective-permute-start(f32[4,8,8,128]{3,2,1,0:T(8,128)S(1)} %get-tuple-element.27), channel_id=1, source_target_pairs={{0,2},{1,3},{2,0},{3,1},{4,6},{5,7},{6,4},{7,5},{8,10},{9,11},{10,... | collective-permute-start | bytes 393224 | tf_op jit(solution)/shard_map/ppermute | solution.py:21
  2.3 1.1 %collective-permute-start.2 = (f32[4,8,8,128]{3,2,1,0:T(8,128)S(1)}, f32[4,8,8,128]{3,2,1,0:T(8,128)S(1)}, u32[]{:S(2)}, u32[]{:S(2)}) collective-permute-start(f32[4,8,8,128]{3,2,1,0:T(8,128)S(1)} %get-tuple-element.28), channel_id=1, source_target_pairs={{0,3},{1,2},{2,1},{3,0},{4,7},{5,6},{6,5},{7,4},{8,11},{9,10},{10,... | collective-permute-start | bytes 393224 | tf_op jit(solution)/shard_map/ppermute | solution.py:21
  3.6 4.1 %shard_map.73 = (f32[1,8,16,128]{3,2,1,0:T(8,128)S(1)}, f32[17,8,16,128]{3,2,1,0:T(8,128)}, f32[14,8,8,128]{3,2,1,0:T(8,128)}, f32[14,8,8,128]{3,2,1,0:T(8,128)}) custom-call(s32[1]{0:T(128)} %bitcast.me_ref._, f32[16,8,16,512]{3,2,1,0:T(8,128)} %a.5), custom_call_target="tpu_custom_call" | custom-call | flops 1024 | bytes 1024 | tf_op jit(solution)/shard_map/pallas_call | solution.py:45
  7.7 1.6 %collective-permute-done.refs_1_.h_ref = f32[2,16,128]{2,1,0:T(8,128)S(1)} collective-permute-done((f32[2,16,128]{2,1,0:T(8,128)S(1)}, f32[2,16,128]{2,1,0:T(8,128)S(1)}, u32[]{:S(2)}, u32[]{:S(2)}) %collective-permute-start) | collective-permute-done | bytes 16416 | tf_op jit(solution)/shard_map/ppermute | solution.py:26
  9.5 1.3 %collective-permute-start.4 = (f32[14,8,8,128]{3,2,1,0:T(8,128)}, f32[14,8,8,128]{3,2,1,0:T(8,128)S(1)}, u32[]{:S(2)}, u32[]{:S(2)}) collective-permute-start(f32[14,8,8,128]{3,2,1,0:T(8,128)} %shard_map.81), channel_id=1, source_target_pairs={{0,2},{1,3},{2,0},{3,1},{4,6},{5,7},{6,4},{7,5},{8,10},{9,11},{10,... | collective-permute-start | bytes 1376264 | tf_op jit(solution)/shard_map/ppermute | solution.py:21
  10.8 0.8 %collective-permute-start.5 = (f32[14,8,8,128]{3,2,1,0:T(8,128)}, f32[14,8,8,128]{3,2,1,0:T(8,128)}, u32[]{:S(2)}, u32[]{:S(2)}) collective-permute-start(f32[14,8,8,128]{3,2,1,0:T(8,128)} %shard_map.82), channel_id=1, source_target_pairs={{0,3},{1,2},{2,1},{3,0},{4,7},{5,6},{6,5},{7,4},{8,11},{9,10},{10,... | collective-permute-start | bytes 1376264 | tf_op jit(solution)/shard_map/ppermute | solution.py:21
  11.9 1.1 %copy-done.4 = f32[32,16,128]{2,1,0:T(8,128)S(1)} copy-done((f32[32,16,128]{2,1,0:T(8,128)S(1)}, f32[32,16,128]{2,1,0:T(8,128)}, u32[]{:S(2)}) %copy-start.4) | copy-done | bytes 262168
  13.0 5.1 %shard_map.77 = (f32[9,32,16,128]{3,2,1,0:T(8,128)S(1)}, f32[8,32,16,128]{3,2,1,0:T(8,128)S(1)}) custom-call(s32[1]{0:T(128)} %bitcast.me_ref._, f32[32,16,128]{2,1,0:T(8,128)S(1)} %copy-done.4, f32[2,16,128]{2,1,0:T(8,128)S(1)} %collective-permute-done.refs_1_.h_ref, s32[16,128]{1,0:T(8,128)S(1)} %broadcast_in_dim.7.act_ref), custom_call_target="tpu_custom_call" | custom-call | flops 1024 | bytes 1024 | tf_op jit(solution)/shard_map/pallas_call | solution.py:45
  18.4 5.4 %shard_map.80 = (f32[16,16,16,128]{3,2,1,0:T(8,128)S(1)}, f32[16,16,128]{2,1,0:T(8,128)S(1)}) custom-call(s32[1]{0:T(128)} %bitcast.me_ref._, f32[16,8,16,512]{3,2,1,0:T(8,128)S(1)} %copy-done, f32[17,8,16,128]{3,2,1,0:T(8,128)S(1)} %collective-permute-done.3.refs_1_, f32[9,32,16,128]{3,2,1,0:T(8,128)S(1)} %get-tuple-element.29.refs_2_.refs_4_, ...), custom_call_target="tpu_custom_call" | custom-call | flops 1024 | bytes 1024 | tf_op jit(solution)/shard_map/pallas_call | solution.py:332
  23.8 1.2 %shard_map.85 = (f32[10,8,8,128]{3,2,1,0:T(8,128)S(1)}, f32[10,8,8,128]{3,2,1,0:T(8,128)S(1)}, f32[4,8,8,128]{3,2,1,0:T(8,128)S(1)}, f32[4,8,8,128]{3,2,1,0:T(8,...) custom-call(s32[1]{0:T(128)} %bitcast.me_ref._, f32[16,8,16,512]{3,2,1,0:T(8,128)} %a.5, ...), custom_call_target="tpu_custom_call" | custom-call | flops 1024 | bytes 1024 | tf_op jit(solution)/shard_map/pallas_call | solution.py:45
  25.0 1.3 %collective-permute-start.12 = (f32[10,8,8,128]{3,2,1,0:T(8,128)S(1)}, f32[10,8,8,128]{3,2,1,0:T(8,128)S(1)}, u32[]{:S(2)}, u32[]{:S(2)}) collective-permute-start(f32[10,8,8,128]{3,2,1,0:T(8,128)S(1)} %get-tuple-element.45), channel_id=1, source_target_pairs={{0,2},{1,3},{2,0},{3,1},{4,6},{5,7},{6,4},{7,5},{8,10},{9,11},{10,... | collective-permute-start | bytes 983048 | tf_op jit(solution)/shard_map/ppermute | solution.py:21
  26.3 2.1 %collective-permute-start.6 = (f32[16,16,128]{2,1,0:T(8,128)S(1)}, f32[16,16,128]{2,1,0:T(8,128)S(1)}, u32[]{:S(2)}, u32[]{:S(2)}) collective-permute-start(f32[16,16,128]{2,1,0:T(8,128)S(1)} %get-tuple-element.36), channel_id=1, source_target_pairs={{4,0},{8,4},{12,8},{16,12},{20,16},{24,20},{28,24},{5,1},{9,5},{13... | collective-permute-start | bytes 393224 | tf_op jit(solution)/shard_map/ppermute | solution.py:31
  29.2 3.8 %collective-permute-done.5.refs_1_ = f32[14,8,8,128]{3,2,1,0:T(8,128)} collective-permute-done((f32[14,8,8,128]{3,2,1,0:T(8,128)}, f32[14,8,8,128]{3,2,1,0:T(8,128)}, u32[]{:S(2)}, u32[]{:S(2)}) %collective-permute-start.5) | collective-permute-done | bytes 458784 | tf_op jit(solution)/shard_map/ppermute | solution.py:21
  33.0 1.2 %collective-permute-done.6.refs_3_.refs_4_ = f32[16,16,128]{2,1,0:T(8,128)S(1)} collective-permute-done((f32[16,16,128]{2,1,0:T(8,128)S(1)}, f32[16,16,128]{2,1,0:T(8,128)S(1)}, u32[]{:S(2)}, u32[]{:S(2)}) %collective-permute-start.6) | collective-permute-done | bytes 131104 | tf_op jit(solution)/shard_map/ppermute | solution.py:31
  34.1 1.1 %shard_map.83.refs_5_.refs_3_ = f32[16,16,128]{2,1,0:T(8,128)S(1)} custom-call(f32[14,8,8,128]{3,2,1,0:T(8,128)S(1)} %collective-permute-done.4.refs_0_, f32[14,8,8,128]{3,2,1,0:T(8,128)} %collective-permute-done.5.refs_1_, f32[8,32,16,128]{3,2,1,0:T(8,128)S(1)} %get-tuple-element.31.refs_2_, f32[16,16,128]{2,1,0:T(8,128)S(1)} %collective-permute-done.6.refs_3_.refs_4_), custom_call_target="tpu_custom_call" | custom-call | flops 1024 | bytes 1024 | tf_op jit(solution)/shard_map/pallas_call | solution.py:45
  35.3 4.0 %shard_map.84 = (f32[16,16,8,128]{3,2,1,0:T(8,128)S(1)}, f32[16,16,128]{2,1,0:T(8,128)S(1)}) custom-call(s32[1]{0:T(128)} %bitcast.me_ref._, f32[14,8,8,128]{3,2,1,0:T(8,128)S(1)} %collective-permute-done.4.refs_0_, f32[14,8,8,128]{3,2,1,0:T(8,128)} %collective-permute-done.5.refs_1_, f32[4,8,8,128]{3,2,1,0:T(8,128)S(1)} %collective-permute-done.1.refs_2_, ...), custom_call_target="tpu_custom_call" | custom-call | flops 1024 | bytes 1024 | tf_op jit(solution)/shard_map/pallas_call | solution.py:332
  39.3 1.9 %collective-permute-start.9 = (f32[16,16,128]{2,1,0:T(8,128)S(1)}, f32[16,16,128]{2,1,0:T(8,128)S(1)}, u32[]{:S(2)}, u32[]{:S(2)}) collective-permute-start(f32[16,16,128]{2,1,0:T(8,128)S(1)} %get-tuple-element.40), channel_id=1, source_target_pairs={{4,0},{8,4},{12,8},{16,12},{20,16},{24,20},{28,24},{5,1},{9,5},{13... | collective-permute-start | bytes 393224 | tf_op jit(solution)/shard_map/ppermute | solution.py:31
  41.4 2.4 %collective-permute-start.11 = (f32[4,8,8,128]{3,2,1,0:T(8,128)S(1)}, f32[4,8,8,128]{3,2,1,0:T(8,128)S(1)}, u32[]{:S(2)}, u32[]{:S(2)}) collective-permute-start(f32[4,8,8,128]{3,2,1,0:T(8,128)S(1)} %get-tuple-element.44), channel_id=1, source_target_pairs={{0,3},{1,2},{2,1},{3,0},{4,7},{5,6},{6,5},{7,4},{8,11},{9,10},{10,... | collective-permute-start | bytes 393224 | tf_op jit(solution)/shard_map/ppermute | solution.py:21
  43.8 2.4 %collective-permute-done.9.refs_5_ = f32[16,16,128]{2,1,0:T(8,128)S(1)} collective-permute-done((f32[16,16,128]{2,1,0:T(8,128)S(1)}, f32[16,16,128]{2,1,0:T(8,128)S(1)}, u32[]{:S(2)}, u32[]{:S(2)}) %collective-permute-start.9) | collective-permute-done | bytes 131104 | tf_op jit(solution)/shard_map/ppermute | solution.py:31
  46.2 3.4 %collective-permute-start.8 = (f32[2,8,8,128]{3,2,1,0:T(8,128)S(1)}, f32[2,8,8,128]{3,2,1,0:T(8,128)S(1)}, u32[]{:S(2)}, u32[]{:S(2)}) collective-permute-start(f32[2,8,8,128]{3,2,1,0:T(8,128)S(1)} %get-tuple-element.39), channel_id=1, source_target_pairs={{0,3},{1,2},{2,1},{3,0},{4,7},{5,6},{6,5},{7,4},{8,11},{9,10},{10,... | collective-permute-start | bytes 196616 | tf_op jit(solution)/shard_map/ppermute | solution.py:21
  49.6 3.8 %shard_map.86.refs_10_ = f32[16,32,16,128]{3,2,1,0:T(8,128)} custom-call(s32[1]{0:T(128)} %bitcast.me_ref._, f32[16,16,16,128]{3,2,1,0:T(8,128)S(1)} %get-tuple-element.33.refs_1_.close_ref, f32[16,16,8,128]{3,2,1,0:T(8,128)S(1)} %get-tuple-element.37.low_ref, f32[10,8,8,128]{3,2,1,0:T(8,128)S(1)} %collective-permute-done.12.refs_0_, ...), custom_call_target="tpu_custom_call" | custom-call | flops 1024 | bytes 1024 | tf_op jit(solution)/shard_map/pallas_call | solution.py:332
  53.5 1.9 %shard_map.87.refs_10_ = f32[16,32,16,128]{3,2,1,0:T(8,128)} custom-call(s32[1]{0:T(128)} %bitcast.me_ref._, f32[16,16,16,128]{3,2,1,0:T(8,128)S(1)} %get-tuple-element.33.refs_1_.close_ref, f32[16,16,8,128]{3,2,1,0:T(8,128)S(1)} %get-tuple-element.37.low_ref, f32[4,8,8,128]{3,2,1,0:T(8,128)S(1)} %collective-permute-done.10.refs_0_, ...), custom_call_target="tpu_custom_call", output_to_operand_aliasing={{}: (13, {})} | custom-call | flops 1024 | bytes 1024 | tf_op jit(solution)/shard_map/pallas_call | solution.py:332
  55.3 1.3 %shard_map.88 = f32[16,32,16,128]{3,2,1,0:T(8,128)} custom-call(s32[1]{0:T(128)} %bitcast.me_ref._, f32[16,16,16,128]{3,2,1,0:T(8,128)S(1)} %get-tuple-element.33.refs_1_.close_ref, f32[16,16,8,128]{3,2,1,0:T(8,128)S(1)} %get-tuple-element.37.low_ref, f32[2,8,8,128]{3,2,1,0:T(8,128)S(1)} %collective-permute-done.7.refs_0_, ...), custom_call_target="tpu_custom_call", output_to_operand_aliasing={{}: (13, {})} | custom-call | flops 1024 | bytes 1024 | tf_op jit(solution)/shard_map/pallas_call | solution.py:332
  (43 shorter events, 1.8 us)
Async XLA Ops:
  0.0 3.4 %copy-start.3 = (f32[32,16,128]{2,1,0:T(8,128)S(1)}, f32[32,16,128]{2,1,0:T(8,128)}, u32[]{:S(2)}) copy-start(f32[32,16,128]{2,1,0:T(8,128)} %c_ref.1) | copy-start | bytes 786436
  1.0 8.3 %collective-permute-start.1 = (f32[4,8,8,128]{3,2,1,0:T(8,128)S(1)}, f32[4,8,8,128]{3,2,1,0:T(8,128)S(1)}, u32[]{:S(2)}, u32[]{:S(2)}) collective-permute-start(f32[4,8,8,128]{3,2,1,0:T(8,128)S(1)} %get-tuple-element.27), channel_id=1, source_target_pairs={{0,2},{1,3},{2,0},{3,1},{4,6},{5,7},{6,4},{7,5},{8,10},{9,11},{10,... | collective-permute-start | bytes 393224 | tf_op jit(solution)/shard_map/ppermute | solution.py:21
  2.3 7.0 %collective-permute-start.2 = (f32[4,8,8,128]{3,2,1,0:T(8,128)S(1)}, f32[4,8,8,128]{3,2,1,0:T(8,128)S(1)}, u32[]{:S(2)}, u32[]{:S(2)}) collective-permute-start(f32[4,8,8,128]{3,2,1,0:T(8,128)S(1)} %get-tuple-element.28), channel_id=1, source_target_pairs={{0,3},{1,2},{2,1},{3,0},{4,7},{5,6},{6,5},{7,4},{8,11},{9,10},{10,... | collective-permute-start | bytes 393224 | tf_op jit(solution)/shard_map/ppermute | solution.py:21
  3.5 5.8 %collective-permute-start = (f32[2,16,128]{2,1,0:T(8,128)S(1)}, f32[2,16,128]{2,1,0:T(8,128)S(1)}, u32[]{:S(2)}, u32[]{:S(2)}) collective-permute-start(f32[2,16,128]{2,1,0:T(8,128)S(1)} %shard_map.74), channel_id=1, source_target_pairs={{0,3},{1,0},{2,1},{3,2},{4,7},{5,4},{6,5},{7,6},{8,11},{9,8},{10,9... | collective-permute-start | bytes 49160 | tf_op jit(solution)/shard_map/ppermute | solution.py:26
  9.3 1.4 %copy-start.1 = (f32[4,8,8,128]{3,2,1,0:T(8,128)}, f32[4,8,8,128]{3,2,1,0:T(8,128)S(1)}, u32[]{:S(2)}) copy-start(f32[4,8,8,128]{3,2,1,0:T(8,128)S(1)} %collective-permute-done.2.refs_3_) | copy-start | bytes 393220
  9.3 2.4 %copy-start.5 = (f32[32,16,128]{2,1,0:T(8,128)S(1)}, f32[32,16,128]{2,1,0:T(8,128)}, u32[]{:S(2)}) copy-start(f32[32,16,128]{2,1,0:T(8,128)} %lat_ref.1) | copy-start | bytes 786436
  9.3 2.4 %copy-start.6 = (f32[32,16,128]{2,1,0:T(8,128)S(1)}, f32[32,16,128]{2,1,0:T(8,128)}, u32[]{:S(2)}) copy-start(f32[32,16,128]{2,1,0:T(8,128)} %mass_ref.1) | copy-start | bytes 786436
  9.3 2.4 %copy-start.7 = (f32[16,128]{1,0:T(8,128)S(1)}, f32[16,128]{1,0:T(8,128)}, u32[]{:S(2)}) copy-start(f32[16,128]{1,0:T(8,128)} %refs_9_.5) | copy-start | bytes 24580
  9.4 2.3 %copy-start.8 = (s32[2,16,128]{2,1,0:T(8,128)S(1)}, s32[2,16,128]{2,1,0:T(8,128)}, u32[]{:S(2)}) copy-start(s32[2,16,128]{2,1,0:T(8,128)} %cloud_ref.1) | copy-start | bytes 49156
  9.4 2.4 %copy-start.9 = (s32[16]{0:T(128)S(1)}, s32[16]{0:T(128)}, u32[]{:S(2)}) copy-start(s32[16]{0:T(128)} %param.13) | copy-start | bytes 196
  9.4 8.7 %collective-permute-start.3 = (f32[17,8,16,128]{3,2,1,0:T(8,128)}, f32[17,8,16,128]{3,2,1,0:T(8,128)S(1)}, u32[]{:S(2)}, u32[]{:S(2)}) collective-permute-start(f32[17,8,16,128]{3,2,1,0:T(8,128)} %shard_map.76), channel_id=1, source_target_pairs={{0,1},{1,0},{2,3},{3,2},{4,5},{5,4},{6,7},{7,6},{8,9},{9,8},{10,11... | collective-permute-start | bytes 3342344 | tf_op jit(solution)/shard_map/ppermute | solution.py:21
  9.5 14.3 %collective-permute-start.4 = (f32[14,8,8,128]{3,2,1,0:T(8,128)}, f32[14,8,8,128]{3,2,1,0:T(8,128)S(1)}, u32[]{:S(2)}, u32[]{:S(2)}) collective-permute-start(f32[14,8,8,128]{3,2,1,0:T(8,128)} %shard_map.81), channel_id=1, source_target_pairs={{0,2},{1,3},{2,0},{3,1},{4,6},{5,7},{6,4},{7,5},{8,10},{9,11},{10,... | collective-permute-start | bytes 1376264 | tf_op jit(solution)/shard_map/ppermute | solution.py:21
  10.8 22.2 %collective-permute-start.5 = (f32[14,8,8,128]{3,2,1,0:T(8,128)}, f32[14,8,8,128]{3,2,1,0:T(8,128)}, u32[]{:S(2)}, u32[]{:S(2)}) collective-permute-start(f32[14,8,8,128]{3,2,1,0:T(8,128)} %shard_map.82), channel_id=1, source_target_pairs={{0,3},{1,2},{2,1},{3,0},{4,7},{5,6},{6,5},{7,4},{8,11},{9,10},{10,... | collective-permute-start | bytes 1376264 | tf_op jit(solution)/shard_map/ppermute | solution.py:21
  11.6 6.8 %copy-start = (f32[16,8,16,512]{3,2,1,0:T(8,128)S(1)}, f32[16,8,16,512]{3,2,1,0:T(8,128)}, u32[]{:S(2)}) copy-start(f32[16,8,16,512]{3,2,1,0:T(8,128)} %a.5) | copy-start | bytes 12582916
  11.9 1.1 %copy-start.4 = (f32[32,16,128]{2,1,0:T(8,128)S(1)}, f32[32,16,128]{2,1,0:T(8,128)}, u32[]{:S(2)}) copy-start(f32[32,16,128]{2,1,0:T(8,128)} %c_ref.1) | copy-start | bytes 786436
  25.0 10.3 %copy-start.2 = (f32[4,8,8,128]{3,2,1,0:T(8,128)S(1)}, f32[4,8,8,128]{3,2,1,0:T(8,128)}, u32[]{:S(2)}) copy-start(f32[4,8,8,128]{3,2,1,0:T(8,128)} %copy-done.1) | copy-start | bytes 393220
  25.0 21.2 %collective-permute-start.12 = (f32[10,8,8,128]{3,2,1,0:T(8,128)S(1)}, f32[10,8,8,128]{3,2,1,0:T(8,128)S(1)}, u32[]{:S(2)}, u32[]{:S(2)}) collective-permute-start(f32[10,8,8,128]{3,2,1,0:T(8,128)S(1)} %get-tuple-element.45), channel_id=1, source_target_pairs={{0,2},{1,3},{2,0},{3,1},{4,6},{5,7},{6,4},{7,5},{8,10},{9,11},{10,... | collective-permute-start | bytes 983048 | tf_op jit(solution)/shard_map/ppermute | solution.py:21
  26.3 7.8 %collective-permute-start.6 = (f32[16,16,128]{2,1,0:T(8,128)S(1)}, f32[16,16,128]{2,1,0:T(8,128)S(1)}, u32[]{:S(2)}, u32[]{:S(2)}) collective-permute-start(f32[16,16,128]{2,1,0:T(8,128)S(1)} %get-tuple-element.36), channel_id=1, source_target_pairs={{4,0},{8,4},{12,8},{16,12},{20,16},{24,20},{28,24},{5,1},{9,5},{13... | collective-permute-start | bytes 393224 | tf_op jit(solution)/shard_map/ppermute | solution.py:31
  28.5 21.2 %collective-permute-start.13 = (f32[10,8,8,128]{3,2,1,0:T(8,128)S(1)}, f32[10,8,8,128]{3,2,1,0:T(8,128)S(1)}, u32[]{:S(2)}, u32[]{:S(2)}) collective-permute-start(f32[10,8,8,128]{3,2,1,0:T(8,128)S(1)} %get-tuple-element.46), channel_id=1, source_target_pairs={{0,3},{1,2},{2,1},{3,0},{4,7},{5,6},{6,5},{7,4},{8,11},{9,10},{10,... | collective-permute-start | bytes 983048 | tf_op jit(solution)/shard_map/ppermute | solution.py:21
  39.3 6.9 %collective-permute-start.9 = (f32[16,16,128]{2,1,0:T(8,128)S(1)}, f32[16,16,128]{2,1,0:T(8,128)S(1)}, u32[]{:S(2)}, u32[]{:S(2)}) collective-permute-start(f32[16,16,128]{2,1,0:T(8,128)S(1)} %get-tuple-element.40), channel_id=1, source_target_pairs={{4,0},{8,4},{12,8},{16,12},{20,16},{24,20},{28,24},{5,1},{9,5},{13... | collective-permute-start | bytes 393224 | tf_op jit(solution)/shard_map/ppermute | solution.py:31
  41.2 12.3 %collective-permute-start.10 = (f32[4,8,8,128]{3,2,1,0:T(8,128)S(1)}, f32[4,8,8,128]{3,2,1,0:T(8,128)S(1)}, u32[]{:S(2)}, u32[]{:S(2)}) collective-permute-start(f32[4,8,8,128]{3,2,1,0:T(8,128)S(1)} %get-tuple-element.43), channel_id=1, source_target_pairs={{0,2},{1,3},{2,0},{3,1},{4,6},{5,7},{6,4},{7,5},{8,10},{9,11},{10,... | collective-permute-start | bytes 393224 | tf_op jit(solution)/shard_map/ppermute | solution.py:21
  41.4 12.1 %collective-permute-start.11 = (f32[4,8,8,128]{3,2,1,0:T(8,128)S(1)}, f32[4,8,8,128]{3,2,1,0:T(8,128)S(1)}, u32[]{:S(2)}, u32[]{:S(2)}) collective-permute-start(f32[4,8,8,128]{3,2,1,0:T(8,128)S(1)} %get-tuple-element.44), channel_id=1, source_target_pairs={{0,3},{1,2},{2,1},{3,0},{4,7},{5,6},{6,5},{7,4},{8,11},{9,10},{10,... | collective-permute-start | bytes 393224 | tf_op jit(solution)/shard_map/ppermute | solution.py:21
  46.2 9.1 %collective-permute-start.7 = (f32[2,8,8,128]{3,2,1,0:T(8,128)S(1)}, f32[2,8,8,128]{3,2,1,0:T(8,128)S(1)}, u32[]{:S(2)}, u32[]{:S(2)}) collective-permute-start(f32[2,8,8,128]{3,2,1,0:T(8,128)S(1)} %get-tuple-element.38), channel_id=1, source_target_pairs={{0,2},{1,3},{2,0},{3,1},{4,6},{5,7},{6,4},{7,5},{8,10},{9,11},{10,... | collective-permute-start | bytes 196616 | tf_op jit(solution)/shard_map/ppermute | solution.py:21
  46.2 9.1 %collective-permute-start.8 = (f32[2,8,8,128]{3,2,1,0:T(8,128)S(1)}, f32[2,8,8,128]{3,2,1,0:T(8,128)S(1)}, u32[]{:S(2)}, u32[]{:S(2)}) collective-permute-start(f32[2,8,8,128]{3,2,1,0:T(8,128)S(1)} %get-tuple-element.39), channel_id=1, source_target_pairs={{0,3},{1,2},{2,1},{3,0},{4,7},{5,6},{6,5},{7,4},{8,11},{9,10},{10,... | collective-permute-start | bytes 196616 | tf_op jit(solution)/shard_map/ppermute | solution.py:21
